TPU v7x, 512 devices: a whole 4x8x8 slice. The times are simulated.
512 devices in a mesh: grp: 16 (over y, z_lo), blk: 32 (over z_hi, x, core).
Axes of the slice: x: 4, y: 8, z: 8 (z_hi: 4, z_lo: 2; z = z_hi * 2 + z_lo), core: 2. Of those that a mesh axis runs over, the one named last changes fastest.
Arguments:
- image: bfloat16 [32, 2048, 1024], P('blk', 'grp')
- text: bfloat16 [32, 2048, 1024], P('blk', 'grp')
- logit_scale: float32 [], replicated, may hold values from 1.5 to 2.5
- lse_row: bfloat16 [32, 2048], P('blk', 'grp')
- lse_col: bfloat16 [32, 2048], P('blk', 'grp')
- pair: int32 [32, 2048], P('blk', 'grp'), may hold values from 0 to 2047, each once within a row
Outputs:
- grad_image: bfloat16 [32, 2048, 1024], P('blk', 'grp')
- grad_text: bfloat16 [32, 2048, 1024], P('blk', 'grp')
Inputs may be any that keep to these rules, and one draw needn't show every extreme that they name: Each row pair[b] is a permutation of 0 .. 2047.
All inputs are finite; a program needn't handle non-finite values.
Results may differ from a plain program's by a relative error of at most 0.022.
Values may be sent and summed in bfloat16 or wider, within the bound.
A program may use at most 64 MiB of HBM per device.

v0:
```python
import jax
import jax.numpy as jnp
from jax import lax
from jax.sharding import PartitionSpec as P

STEPS = 2


def shifted(block, axis, distance):
    devices = range(lax.axis_size(axis))
    route = [((i - distance) % len(devices), i) for i in devices]
    return lax.ppermute(block, axis, route)


def score_grad(img, lrow, txt, lcol, pairs, scale, own):
    scores = (
        lax.dot_general(img, txt, (((1,), (1,)), ((), ())), preferred_element_type=jnp.float32)
        * scale
    )
    row_lse = lrow.astype(jnp.float32)
    col_lse = lcol.astype(jnp.float32)
    dscore = 0.5 * (jnp.exp(scores - row_lse[:, None]) + jnp.exp(scores - col_lse[None, :]))
    if own:
        columns = jnp.arange(txt.shape[0], dtype=jnp.int32)
        dscore = dscore - (pairs[:, None] == columns[None, :]).astype(jnp.float32)
    return dscore.astype(jnp.bfloat16)


def text_term(dscore, img):
    return lax.dot_general(
        dscore, img, (((0,), (0,)), ((), ())), preferred_element_type=jnp.float32
    )


def body(image, text, logit_scale, lse_row, lse_col, pair):
    rows_dev = image.shape[1]
    width = image.shape[2]
    text_all, lcol_all = (
        lax.all_gather(text, "grp", axis=1, tiled=True),
        lax.all_gather(lse_col, "grp", axis=1, tiled=True),
    )
    txt = text_all[0]
    lcol = lcol_all[0]
    own_img = image[0]
    own_lrow = lse_row[0]
    own_pairs = pair[0]
    text_acc = jnp.zeros((txt.shape[0], width), jnp.float32)
    pieces = []
    moving_img, moving_lrow = (own_img, own_lrow)
    for step in range(STEPS):
        if step > 0:
            moving_img, moving_lrow = shifted((moving_img, moving_lrow), "blk", 1)
        dscore = score_grad(moving_img, moving_lrow, txt, lcol, own_pairs, logit_scale, step == 0)
        pieces.append(logit_scale * jnp.dot(dscore, txt, preferred_element_type=jnp.float32))
        text_acc = text_acc + logit_scale * text_term(dscore, moving_img)
    image_acc = pieces[STEPS - 1]
    step = 0
    image_acc = (
        shifted(image_acc.astype(jnp.bfloat16), "blk", -1).astype(image_acc.dtype) + pieces[step]
    )
    shares = lax.optimization_barrier(text_acc.astype(jnp.bfloat16)).astype(jnp.float32)
    summed = lax.psum(shares.astype(jnp.bfloat16), "grp").astype(jnp.float32)
    text_rows = lax.dynamic_slice_in_dim(summed, lax.axis_index("grp") * rows_dev, rows_dev, 0)
    grad_image = image_acc.astype(jnp.bfloat16)[None]
    grad_text = text_rows.astype(jnp.bfloat16)[None]
    return (grad_image, grad_text)


def solution(mesh):
    return jax.shard_map(
        body,
        mesh=mesh,
        in_specs=(
            P("blk", "grp", None),
            P("blk", "grp", None),
            P(),
            P("blk", "grp"),
            P("blk", "grp"),
            P("blk", "grp"),
        ),
        out_specs=(P("blk", "grp", None), P("blk", "grp", None)),
        check_vma=False,
    )
```

profile of v0, /device:TPU:6, one launch (start us, length us, event | category | flops | bytes accessed | tf_op | source)
XLA Modules:
  0.0 340.9 jit_solution(10496087822701037526)
XLA Ops:
  7.2 0.0 copy-start.1
  7.2 0.0 all-gather.2.cloned.1.call-start
  7.2 0.7 all-gather.2.cloned.1.call-update
  7.9 0.0 all-reduce.2.cloned.1.call-start
  8.0 1.9 collective-permute-start
  9.9 6.1 %collective-permute-start.1 = (bf16[128]{0:T(256)(128)(2,1)}, bf16[128]{0:T(256)(128)(2,1)S(1)}, u32[]{:S(2)}, u32[]{:S(2)}) collective-permute-start(bf16[128]{0:T(256)(128)(2,1)} %bitcast.47), channel_id=1, source_target_pairs={{31,0},{0,1},{1,2},{2,3},{3,4},{4,5},{5,6},{6,7},{7,8},{8,9},{9,10... | collective-permute-start | bytes 776 | tf_op jit(solution)/shard_map/ppermute | solution.py:12
  16.0 0.7 bitcast_convert_fusion
  16.7 35.0 %all_gather.7 = bf16[1,2048]{1,0:T(2,128)(2,1)S(1)} all-gather(bf16[1,128]{1,0:T(2,128)(2,1)} %param.10), channel_id=1, replica_groups=mesh['grp'=16,'blk'=32] {'grp'}, dimensions={1}, use_global_device_ids=true | all-gather | bytes 4352 | tf_op jit(solution)/shard_map/all_gather | solution.py:40
  52.4 0.0 collective-permute-done.1
  52.4 64.5 %all-gather.2.cloned.1.call-done = bf16[1,2048,1024]{2,1,0:T(8,128)(2,1)} async-done(((bf16[1,128,1024]{2,1,0:T(8,128)(2,1)}), bf16[1,2048,1024]{2,1,0:T(8,128)(2,1)}) %all-gather.2.cloned.1.call-update) | async-done | bytes 4194320 | tf_op jit(solution)/shard_map/all_gather | solution.py:39
  116.9 4.0 %subtract_convert_fusion = bf16[128,2048]{1,0:T(8,128)(2,1)S(1)} fusion(bf16[1,2048,1024]{2,1,0:T(8,128)(2,1)} %all-gather.2.cloned.1.call-done, s32[128]{0:T(128)} %bitcast.48, f32[128]{0:T(128)S(1)} %bitcast_convert_fusion, f32[2048]{0:T(1024)S(1)} %bitcast.45, f32[]{:T(128)S(6)} %copy.9, bf16[1,128,1024]{2,1,0:T(8,128)(2,1)} %param.6), kind=kOutput, calls=%fused_computation.14 | convolution fusion | flops 539230208 | bytes 4989956 | tf_op jit(solution)/shard_map/dot_general | solution.py:17
  120.9 0.0 copy-done.1
  120.9 1.3 fusion.31
  122.2 0.0 collective-permute-done
  122.2 0.9 copy-done
  123.1 1.7 multiply_convert_fusion.1
  124.8 3.3 multiply_convert_fusion
  128.1 0.0 all-reduce.2.cloned.1.call-update
  128.1 2.9 fusion.20
  131.0 1.9 collective-permute-start.2
  132.9 3.9 %collective-permute-done.2 = bf16[128,1024]{1,0:T(8,128)(2,1)S(1)} collective-permute-done((bf16[128,1024]{1,0:T(8,128)(2,1)S(1)}, bf16[128,1024]{1,0:T(8,128)(2,1)S(1)}, u32[]{:S(2)}, u32[]{:S(2)}) %collective-permute-start.2) | collective-permute-done | bytes 262176 | tf_op jit(solution)/shard_map/ppermute | solution.py:12
  136.8 3.6 %fusion.27 = bf16[1,128,1024]{2,1,0:T(8,128)(2,1)} fusion(bf16[128,1024]{1,0:T(8,128)(2,1)S(1)} %collective-permute-done.2, bf16[128,2048]{1,0:T(8,128)(2,1)S(1)} %subtract_convert_fusion, bf16[1,2048,1024]{2,1,0:T(8,128)(2,1)} %all-gather.2.cloned.1.call-done, f32[]{:T(128)S(6)} %copy.9), kind=kOutput, calls=%fused_computation.19 | convolution fusion | flops 537395200 | bytes 5242884 | tf_op jit(solution)/shard_map/dot_general | solution.py:54
  140.4 192.0 %all-reduce.2.cloned.1.call-done = bf16[2048,1024]{1,0:T(8,128)(2,1)} async-done(((bf16[2048,1024]{1,0:T(8,128)(2,1)}), bf16[2048,1024]{1,0:T(8,128)(2,1)}) %all-reduce.2.cloned.1.call-update) | async-done | bytes 4194320 | tf_op jit(solution)/shard_map/psum | solution.py:62
  332.4 1.7 fusion.28
  (3 shorter events, 0.0 us)
Async XLA Ops:
  7.2 113.7 %copy-start.1 = (bf16[1,128,1024]{2,1,0:T(8,128)(2,1)S(1)}, bf16[1,128,1024]{2,1,0:T(8,128)(2,1)}, u32[]{:S(2)}) copy-start(bf16[1,128,1024]{2,1,0:T(8,128)(2,1)} %param.6) | copy-start | bytes 786436
  7.2 109.7 %all-gather.2.cloned.1.call-start = ((), (), s32[]{:S(2)}) async-start(), calls=%async_computation | async-start | bytes 4456448 | tf_op jit(solution)/shard_map/all_gather | solution.py:39
  7.9 324.5 %all-reduce.2.cloned.1.call-start = ((), (), s32[]{:S(2)}) async-start(), calls=%async_computation.1 | async-start | bytes 8388608 | tf_op jit(solution)/shard_map/psum | solution.py:62
  8.0 114.2 %collective-permute-start = (bf16[128,1024]{1,0:T(8,128)(2,1)}, bf16[128,1024]{1,0:T(8,128)(2,1)S(1)}, u32[]{:S(2)}, u32[]{:S(2)}) collective-permute-start(bf16[128,1024]{1,0:T(8,128)(2,1)} %bitcast.44), channel_id=1, source_target_pairs={{31,0},{0,1},{1,2},{2,3},{3,4},{4,5},{5,6},{6,7},{7,8},{8,9},{9,10... | collective-permute-start | bytes 786440 | tf_op jit(solution)/shard_map/ppermute | solution.py:12
  9.9 42.5 %collective-permute-start.1 = (bf16[128]{0:T(256)(128)(2,1)}, bf16[128]{0:T(256)(128)(2,1)S(1)}, u32[]{:S(2)}, u32[]{:S(2)}) collective-permute-start(bf16[128]{0:T(256)(128)(2,1)} %bitcast.47), channel_id=1, source_target_pairs={{31,0},{0,1},{1,2},{2,3},{3,4},{4,5},{5,6},{6,7},{7,8},{8,9},{9,10... | collective-permute-start | bytes 776 | tf_op jit(solution)/shard_map/ppermute | solution.py:12
  120.9 2.2 copy-start
  131.0 5.8 %collective-permute-start.2 = (bf16[128,1024]{1,0:T(8,128)(2,1)S(1)}, bf16[128,1024]{1,0:T(8,128)(2,1)S(1)}, u32[]{:S(2)}, u32[]{:S(2)}) collective-permute-start(bf16[128,1024]{1,0:T(8,128)(2,1)S(1)} %fusion.20), channel_id=1, source_target_pairs={{1,0},{2,1},{3,2},{4,3},{5,4},{6,5},{7,6},{8,7},{9,8},{10,9},{11,1... | collective-permute-start | bytes 786440 | tf_op jit(solution)/shard_map/ppermute | solution.py:12
Sparse Core Ops, SparseCore 0:
  10.1 106.7 all-gather.1
  128.2 204.1 all-reduce.1
where the time goes:
time: 341 us
  waiting for transfers between devices  261 us (77%)
  blocking collectives  35 us (10%)
  matrix products  16.8 us (5%)
  between operations  14.8 us (4%)
  starting transfers between devices  10 us (3%)
    psum x1, waiting for transfers between devices, body(): summed = lax.psum(shares.astype(jnp.bfloat16), 'grp').astype(jnp.float32)  192 us
    all_gather x1, waiting for transfers between devices, body(): lax.all_gather(text, 'grp', axis=1, tiled=True)  64.5 us
    all_gather x1, blocking collectives, body(): lax.all_gather(lse_col, 'grp', axis=1, tiled=True)  35 us
    ppermute x3, starting transfers between devices, shifted(): return lax.ppermute(block, axis, route)  9.95 us
  transfers between devices with their start and end apart: 5, of which 3 were waited for; matrix products, arithmetic and copies ran while one was open for 4% of the time, Pallas kernels for 0%

commit v1 on v0

v1 whole, which is shorter than its diff:
```python
import functools

import jax
import jax.numpy as jnp
from jax import lax
from jax.experimental import pallas as pl
from jax.experimental.pallas import tpu as pltpu
from jax.sharding import PartitionSpec as P

MESH = pl.DeviceIdType.MESH
RING = 8
ROWS = 128
PARTS = 4
CHUNK = ROWS // PARTS
HALF = PARTS // 2
PLACES = 8
NEAR = ((0, 1), (2, 3))
F32 = jnp.float32
BF16 = jnp.bfloat16


def place(direction, hops):
    return 0 if hops == 0 else 7 if hops == 4 else 2 * hops - 1 + direction


def gather_order(direction):
    first, second = NEAR[direction], NEAR[1 - direction]
    order = [(hop, part) for hop in (1, 2, 3) for part in first + second]
    return order + [(4, part) for part in first]


def reduce_order(direction):
    far, near = NEAR[direction], NEAR[1 - direction]
    order = [(3, near), (4, far), (2, near), (3, far), (1, near), (2, far), (1, far)]
    return [(hops, part) for hops, parts in order for part in parts]


def kernel(
    image, text, scale_ref, lrow_ref, lcol_ref, pair_ref, gi_out, gt_out,
    txt, img, meta, col, lct, dt, ct, rsend, rrecv, g0, gis, gir, zs, zr, oi, ot,
    local_sem, out_sem, ag_s, ag_r, rs_s, rs_r, im_s, im_r, me_s, me_r, co_s, co_r, gi_s, gi_r, zz_s, zz_r,
):
    g = lax.axis_index("grp")
    b = lax.axis_index("blk")
    n_blk = lax.axis_size("blk")
    n_grp = 2 * RING
    zpart = g + 1 - 2 * lax.rem(g, 2)
    nxt = lax.rem(b + 1, n_blk)
    prv = lax.rem(b + n_blk - 1, n_blk)
    ring = [lax.rem(g + 2 * i, n_grp) for i in range(RING)]
    side = [ring[1], ring[7]]
    scale = scale_ref[0]

    def send(src, dst, s_sem, r_sem, **to):
        copy = pltpu.make_async_remote_copy(
            src_ref=src, dst_ref=dst, send_sem=s_sem, recv_sem=r_sem,
            device_id={"grp": to.get("grp", g), "blk": to.get("blk", b)}, device_id_type=MESH,
        )
        return copy

    own_txt = pltpu.make_async_copy(text.at[0], txt.at[pl.ds(0, ROWS)], local_sem.at[0])
    own_img = pltpu.make_async_copy(image.at[0], img.at[pl.ds(0, ROWS)], local_sem.at[1])
    own_txt.start()
    own_img.start()

    barrier = pltpu.get_barrier_semaphore()
    for i in range(1, RING):
        pl.semaphore_signal(barrier, inc=1, device_id={"grp": ring[i], "blk": b}, device_id_type=MESH)
    pl.semaphore_signal(barrier, inc=1, device_id={"grp": zpart, "blk": b}, device_id_type=MESH)
    pl.semaphore_signal(barrier, inc=1, device_id={"grp": g, "blk": nxt}, device_id_type=MESH)
    pl.semaphore_signal(barrier, inc=1, device_id={"grp": g, "blk": prv}, device_id_type=MESH)

    meta[0] = jnp.zeros((8, ROWS), F32)
    meta[0, 0:1, :] = lrow_ref[...].astype(F32)
    meta[0, 1:2, :] = pair_ref[...].astype(F32)
    col[0] = jnp.broadcast_to(lcol_ref[...].astype(F32), (8, ROWS))
    own_txt.wait()
    own_img.wait()
    pl.semaphore_wait(barrier, RING - 1 + 3)

    started = []

    def go(copy):
        copy.start()
        started.append(copy)
        return copy

    orders = [gather_order(0), gather_order(1)]

    def gather_copy(direction, n):
        hop, part = orders[direction][n]
        rows = lambda p: txt.at[pl.ds(p * ROWS + part * CHUNK, CHUNK)]
        return send(
            rows(place(direction, hop - 1)), rows(place(direction, hop)),
            ag_s.at[direction, n], ag_r.at[direction, n], grp=side[direction],
        )

    gather = [[gather_copy(d, n) for n in range(len(orders[d]))] for d in range(2)]
    for n in range(PARTS):
        for d in range(2):
            go(gather[d][n])

    half = ROWS // 2
    z_img = go(send(img.at[pl.ds(0, ROWS)], img.at[pl.ds(ROWS, ROWS)], im_s.at[0], im_r.at[0], grp=zpart))
    z_meta = go(send(meta.at[0], meta.at[1], me_s.at[0], me_r.at[0], grp=zpart))
    x_img = go(send(img.at[pl.ds(0, ROWS)], img.at[pl.ds(2 * ROWS, ROWS)], im_s.at[1], im_r.at[1], blk=nxt))
    x_meta = go(send(meta.at[0], meta.at[2], me_s.at[1], me_r.at[1], blk=nxt))
    cols = []
    for i in range(1, RING):
        there = 7 if i == 4 else 2 * i - 1 if i < 4 else 2 * (RING - i)
        cols.append(go(send(col.at[0], col.at[there], co_s.at[i - 1], co_r.at[there - 1], grp=ring[i])))

    def arrived(n):
        for d in range(2):
            gather[d][n].wait_recv()
            if n + PARTS < len(orders[d]):
                go(gather[d][n + PARTS])

    def scores(p0, count, k):
        t = txt[p0 * ROWS : (p0 + count) * ROWS, :]
        s = lax.dot_general(
            t, img[k * 2 * ROWS : (k + 1) * 2 * ROWS, :], (((1,), (1,)), ((), ())), preferred_element_type=F32
        )
        lr = jnp.concatenate([meta[2 * k, 0:1, :], meta[2 * k + 1, 0:1, :]], axis=1)
        for i in range(count):
            p = p0 + i
            si = s[i * ROWS : (i + 1) * ROWS] * scale
            if k == 0:
                lct[p * ROWS : (p + 1) * ROWS, :] = jnp.broadcast_to(col[p, 0:1, :], (ROWS, ROWS)).T
            lc = lct[p * ROWS : (p + 1) * ROWS, :]
            lc = jnp.concatenate([lc, lc], axis=1)
            d = 0.5 * (jnp.exp(si - lr) + jnp.exp(si - lc))
            if k == 0:
                rel = 0 if p == 0 else 4 if p == 7 else (RING - (p + 1) // 2) if p % 2 else p // 2
                pr = jnp.concatenate([meta[0, 1:2, :], meta[1, 1:2, :]], axis=1).astype(jnp.int32)
                row = ring[rel] * ROWS + lax.broadcasted_iota(jnp.int32, (ROWS, 2 * ROWS), 0)
                d = d - (pr == row).astype(F32)
            dt[p * ROWS : (p + 1) * ROWS, k * 2 * ROWS : (k + 1) * 2 * ROWS] = d.astype(BF16)

    def contribution(p0, count):
        rows = slice(p0 * ROWS, (p0 + count) * ROWS)
        ct[rows, :] = jnp.dot(dt[rows, :], img[...], preferred_element_type=F32)

    def image_term(k):
        return lax.dot_general(
            dt[:, k * 2 * ROWS : (k + 1) * 2 * ROWS], txt[...], (((0,), (0,)), ((), ())), preferred_element_type=F32
        )

    r_orders = [reduce_order(0), reduce_order(1)]

    def reduce_copy(direction, n):
        rows = pl.ds(n * CHUNK, CHUNK)
        return send(
            rsend.at[direction, rows], rrecv.at[direction, rows],
            rs_s.at[direction, n], rs_r.at[direction, n], grp=side[direction],
        )

    reduction = [[reduce_copy(d, n) for n in range(len(r_orders[d]))] for d in range(2)]

    def reduce_step(n):
        for d in range(2):
            hops, part = r_orders[d][n]
            start = place(1 - d, hops) * ROWS + part * CHUNK
            total = ct[start : start + CHUNK, :]
            if (hops + 1, part) in r_orders[d]:
                m = r_orders[d].index((hops + 1, part))
                reduction[d][m].wait_recv()
                total = total + rrecv[d, m * CHUNK : (m + 1) * CHUNK, :].astype(F32)
            rsend[d, n * CHUNK : (n + 1) * CHUNK, :] = total.astype(BF16)
            go(reduction[d][n])

    for n in range(4):
        arrived(n)
    z_img.wait_recv()
    z_meta.wait_recv()
    x_img2 = go(send(img.at[pl.ds(ROWS, ROWS)], img.at[pl.ds(3 * ROWS, ROWS)], im_s.at[2], im_r.at[2], blk=nxt))
    x_meta2 = go(send(meta.at[1], meta.at[3], me_s.at[2], me_r.at[2], blk=nxt))
    for copy in cols:
        copy.wait_recv()
    scores(0, 1, 0)
    arrived(4)
    scores(1, 2, 0)
    for n in (5, 6, 7):
        arrived(n)
    scores(3, 2, 0)
    arrived(8)
    arrived(9)
    for copy in (x_img, x_meta, x_img2, x_meta2):
        copy.wait_recv()
    scores(0, 1, 1)
    scores(1, 2, 1)
    arrived(10)
    scores(3, 2, 1)
    contribution(0, 1)
    arrived(11)
    scores(5, 2, 0)
    scores(5, 2, 1)
    contribution(5, 2)
    reduce_step(0)
    reduce_step(1)
    arrived(12)
    arrived(13)
    scores(7, 1, 0)
    scores(7, 1, 1)
    contribution(7, 1)
    reduce_step(2)
    reduce_step(3)

    gis[...] = image_term(1).astype(BF16)
    back = [
        go(send(gis.at[rows], gir.at[rows], gi_s.at[i], gi_r.at[i], blk=prv))
        for i, rows in enumerate((pl.ds(ROWS, ROWS), pl.ds(0, ROWS)))
    ]
    contribution(3, 2)
    reduce_step(4)
    reduce_step(5)
    contribution(1, 2)
    g0[...] = image_term(0)
    for n in (6, 7, 8, 9):
        reduce_step(n)
    back[0].wait_recv()
    zs[...] = (g0[ROWS:, :] + gir[ROWS:, :].astype(F32)).astype(BF16)
    z_grad = go(send(zs, zr, zz_s, zz_r, grp=zpart))
    back[1].wait_recv()
    for n in (10, 11):
        reduce_step(n)
    z_grad.wait_recv()
    oi[...] = (scale * (g0[:ROWS, :] + gir[:ROWS, :].astype(F32) + zr[...].astype(F32))).astype(BF16)
    out_i = pltpu.make_async_copy(oi, gi_out.at[0], out_sem.at[0])
    out_i.start()
    for n in (12, 13):
        reduce_step(n)
    for part in NEAR[1] + NEAR[0]:
        total = ct[part * CHUNK : (part + 1) * CHUNK, :]
        for d in range(2):
            m = r_orders[d].index((1, part))
            reduction[d][m].wait_recv()
            total = total + rrecv[d, m * CHUNK : (m + 1) * CHUNK, :].astype(F32)
        ot[part * CHUNK : (part + 1) * CHUNK, :] = (scale * total).astype(BF16)
    out_t = pltpu.make_async_copy(ot, gt_out.at[0], out_sem.at[1])
    out_t.start()
    for copy in started:
        copy.wait_send()
    out_i.wait()
    out_t.wait()


def body(image, text, logit_scale, lse_row, lse_col, pair):
    width = image.shape[2]
    msgs = 3 * PARTS + HALF
    any_spec = pl.BlockSpec(memory_space=pl.ANY)
    vmem = pl.BlockSpec(memory_space=pltpu.VMEM)
    dma = pltpu.SemaphoreType.DMA
    out = jax.ShapeDtypeStruct((1, ROWS, width), BF16)
    return pl.pallas_call(
        kernel,
        out_shape=(out, out),
        in_specs=[any_spec, any_spec, pl.BlockSpec(memory_space=pltpu.SMEM), vmem, vmem, vmem],
        out_specs=(any_spec, any_spec),
        scratch_shapes=[
            pltpu.VMEM((PLACES * ROWS, width), BF16),
            pltpu.VMEM((4 * ROWS, width), BF16),
            pltpu.VMEM((4, 8, ROWS), F32),
            pltpu.VMEM((PLACES, 8, ROWS), F32),
            pltpu.VMEM((PLACES * ROWS, ROWS), F32),
            pltpu.VMEM((PLACES * ROWS, 4 * ROWS), BF16),
            pltpu.VMEM((PLACES * ROWS, width), F32),
            pltpu.VMEM((2, msgs * CHUNK, width), BF16),
            pltpu.VMEM((2, msgs * CHUNK, width), BF16),
            pltpu.VMEM((2 * ROWS, width), F32),
            pltpu.VMEM((2 * ROWS, width), BF16),
            pltpu.VMEM((2 * ROWS, width), BF16),
            pltpu.VMEM((ROWS, width), BF16),
            pltpu.VMEM((ROWS, width), BF16),
            pltpu.VMEM((ROWS, width), BF16),
            pltpu.VMEM((ROWS, width), BF16),
            dma((2,)),
            dma((2,)),
            dma((2, msgs)),
            dma((2, msgs)),
            dma((2, msgs)),
            dma((2, msgs)),
            dma((3,)),
            dma((3,)),
            dma((3,)),
            dma((3,)),
            dma((RING - 1,)),
            dma((RING - 1,)),
            dma((2,)),
            dma((2,)),
            dma,
            dma,
        ],
        compiler_params=pltpu.CompilerParams(
            collective_id=0, has_side_effects=True, vmem_limit_bytes=48 * 2**20
        ),
        cost_estimate=pl.CostEstimate(
            flops=12 * ROWS * 16 * ROWS * width, bytes_accessed=8 * ROWS * width, transcendentals=8 * ROWS * 16 * ROWS
        ),
    )(image, text, jnp.reshape(logit_scale, (1,)), lse_row, lse_col, pair)


def solution(mesh):
    return jax.shard_map(
        body,
        mesh=mesh,
        in_specs=(
            P("blk", "grp", None),
            P("blk", "grp", None),
            P(),
            P("blk", "grp"),
            P("blk", "grp"),
            P("blk", "grp"),
        ),
        out_specs=(P("blk", "grp", None), P("blk", "grp", None)),
        check_vma=False,
    )
```

time: 341 us -> 64.9 us (0.19)
  the two profiles are of different devices: /device:TPU:6 before, /device:TPU:16 now
where the time goes in v1:
time: 64.9 us; the launch traced here: 64.7 us
  Pallas kernels  59.4 us (92%)
  local copies, waits for them, and re-layouts  3.97 us (6%)
  between operations  1.31 us (2%)
    pallas_call x1, Pallas kernels, body(): pl.pallas_call(kernel, out_shape=(out, out), in_specs=[any_spec, any_spec...  59.4 us
    unnamed x12, local copies, waits for them, and re-layouts  3.97 us

profile of v1, /device:TPU:16, one launch (start us, length us, event | category | flops | bytes accessed | tf_op | source)
XLA Modules:
  0.0 64.7 jit_solution(1063855829638932327)
XLA Ops:
  1.3 0.0 copy-start.2
  1.3 0.0 copy-start.3
  1.3 0.0 copy-start.4
  1.3 0.6 copy-done.2
  1.9 0.0 copy-done.3
  1.9 0.0 copy-done.4
  2.0 0.0 copy-start
  2.0 0.9 %copy-done = bf16[1,128,1024]{2,1,0:T(8,128)(2,1)S(1)} copy-done((bf16[1,128,1024]{2,1,0:T(8,128)(2,1)S(1)}, bf16[1,128,1024]{2,1,0:T(8,128)(2,1)}, u32[]{:S(2)}) %copy-start) | copy-done | bytes 262168
  2.9 0.0 copy-start.1
  2.9 0.9 %copy-done.1 = bf16[1,128,1024]{2,1,0:T(8,128)(2,1)S(1)} copy-done((bf16[1,128,1024]{2,1,0:T(8,128)(2,1)S(1)}, bf16[1,128,1024]{2,1,0:T(8,128)(2,1)}, u32[]{:S(2)}) %copy-start.1) | copy-done | bytes 262168
  3.9 59.4 %shard_map.77 = (bf16[1,128,1024]{2,1,0:T(8,128)(2,1)S(1)}, bf16[1,128,1024]{2,1,0:T(8,128)(2,1)S(1)}) custom-call(bf16[1,128,1024]{2,1,0:T(8,128)(2,1)S(1)} %copy-done, bf16[1,128,1024]{2,1,0:T(8,128)(2,1)S(1)} %copy-done.1, f32[1]{0:T(128)} %bitcast.1.scale_ref, bf16[1,128]{1,0:T(2,128)(2,1)S(1)} %copy-done.2, bf16[1,128]{1,0:T(2,128)(2,1)S(1)} %copy-done.3, ...), custom_call_target="tpu_custom_call" | custom-call | flops 3221225472 | bytes 1048576 | tf_op jit(solution)/shard_map/pallas_call | solution.py:255
  63.3 0.7 %copy.11 = bf16[1,128,1024]{2,1,0:T(8,128)(2,1)} copy(bf16[1,128,1024]{2,1,0:T(8,128)(2,1)S(1)} %get-tuple-element.4) | data formatting | bytes 524288
  64.0 0.7 %copy.12 = bf16[1,128,1024]{2,1,0:T(8,128)(2,1)} copy(bf16[1,128,1024]{2,1,0:T(8,128)(2,1)S(1)} %get-tuple-element.5) | data formatting | bytes 524288
Async XLA Ops:
  1.3 0.7 %copy-start.2 = (bf16[1,128]{1,0:T(2,128)(2,1)S(1)}, bf16[1,128]{1,0:T(2,128)(2,1)}, u32[]{:S(2)}) copy-start(bf16[1,128]{1,0:T(2,128)(2,1)} %lrow_ref.1) | copy-start | bytes 772
  1.3 0.7 %copy-start.3 = (bf16[1,128]{1,0:T(2,128)(2,1)S(1)}, bf16[1,128]{1,0:T(2,128)(2,1)}, u32[]{:S(2)}) copy-start(bf16[1,128]{1,0:T(2,128)(2,1)} %lcol_ref.1) | copy-start | bytes 772
  1.3 0.7 %copy-start.4 = (s32[1,128]{1,0:T(1,128)S(1)}, s32[1,128]{1,0:T(1,128)}, u32[]{:S(2)}) copy-start(s32[1,128]{1,0:T(1,128)} %pair_ref.1) | copy-start | bytes 1540
  2.0 0.9 %copy-start = (bf16[1,128,1024]{2,1,0:T(8,128)(2,1)S(1)}, bf16[1,128,1024]{2,1,0:T(8,128)(2,1)}, u32[]{:S(2)}) copy-start(bf16[1,128,1024]{2,1,0:T(8,128)(2,1)} %image.1) | copy-start | bytes 786436
  2.9 0.9 %copy-start.1 = (bf16[1,128,1024]{2,1,0:T(8,128)(2,1)S(1)}, bf16[1,128,1024]{2,1,0:T(8,128)(2,1)}, u32[]{:S(2)}) copy-start(bf16[1,128,1024]{2,1,0:T(8,128)(2,1)} %text.1) | copy-start | bytes 786436

commit v2 on v0

v2 whole, which is shorter than its diff:
```python
import functools

import jax
import jax.numpy as jnp
from jax import lax
from jax.experimental import pallas as pl
from jax.experimental.pallas import tpu as pltpu
from jax.sharding import PartitionSpec as P

MESH = pl.DeviceIdType.MESH
RING = 8
ROWS = 128
PARTS = 4
CHUNK = ROWS // PARTS
HALF = ROWS // 2
PLACES = 8
RUN = 8
FAR = ((2, 3), (1, 0))
F32 = jnp.float32
BF16 = jnp.bfloat16


def place(direction, hops):
    return 0 if hops == 0 else 7 if hops == 4 else 2 * hops - 1 + direction


def gather_order(direction):
    far, near = FAR[direction], FAR[1 - direction]
    order = [(hop, part) for hop in (1, 2, 3) for part in far + near]
    return order + [(4, part) for part in far]


def reduce_order(direction):
    f0, f1 = FAR[direction]
    n0, n1 = FAR[1 - direction]
    return [
        (3, n0), (3, n1), (4, f0), (4, f1), (2, n0), (3, f0), (3, f1),
        (2, n1), (2, f0), (2, f1), (1, n0), (1, f0), (1, f1), (1, n1),
    ]


def kernel(
    image, text, scale_ref, lrow_ref, lcol_ref, pair_ref, gi_out, gt_out,
    txt, img, meta, col, lct, dt, ct, rsend, rrecv, g0, g1, gis, gir, zs, zr, vecs, pairs, oi, ot,
    local_sem, out_sem, ag_s, ag_r, rs_s, rs_r, im_s, im_r, me_s, me_r, co_s, co_r, gi_s, gi_r, zz_s, zz_r,
):
    g = lax.axis_index("grp")
    b = lax.axis_index("blk")
    n_blk = lax.axis_size("blk")
    n_grp = 2 * RING
    zpart = g + 1 - 2 * lax.rem(g, 2)
    nxt = lax.rem(b + 1, n_blk)
    prv = lax.rem(b + n_blk - 1, n_blk)
    ring = [lax.rem(g + 2 * i, n_grp) for i in range(RING)]
    side = [ring[1], ring[7]]
    z_lo = lax.rem(g, 2)
    last = lax.rem(b, RUN) == RUN - 1
    first = lax.rem(b, RUN) == 0
    zero = b == 0
    has_next = jnp.logical_not(jnp.logical_and(last, z_lo == 0))
    has_prev = jnp.logical_not(jnp.logical_and(first, z_lo == 1))
    outlet = jnp.logical_and(last, z_lo == 1)
    inlet = jnp.logical_and(first, z_lo == 0)
    next_grp = jnp.where(last, zpart, g)
    prev_grp = jnp.where(first, zpart, g)

    barrier = pltpu.get_barrier_semaphore()

    def greet(grp, blk):
        pl.semaphore_signal(barrier, inc=1, device_id={"grp": grp, "blk": blk}, device_id_type=MESH)

    greet(side[0], b)
    greet(side[1], b)
    greet(zpart, b)

    @pl.when(has_prev)
    def _():
        greet(prev_grp, prv)

    def copy_to(src, dst, s_sem, r_sem, grp=g, blk=b):
        return pltpu.make_async_remote_copy(
            src_ref=src, dst_ref=dst, send_sem=s_sem, recv_sem=r_sem,
            device_id={"grp": grp, "blk": blk}, device_id_type=MESH,
        )

    local = [
        pltpu.make_async_copy(src, dst, local_sem.at[i])
        for i, (src, dst) in enumerate((
            (pair_ref, pairs),
            (lrow_ref, vecs.at[0]),
            (lcol_ref, vecs.at[1]),
            (text.at[0], txt.at[pl.ds(0, ROWS)]),
            (image.at[0], img.at[pl.ds(0, ROWS)]),
        ))
    ]
    for copy in local:
        copy.start()
    scale = scale_ref[0]
    started = []

    def go(copy):
        copy.start()
        started.append(copy)
        return copy

    orders = [gather_order(0), gather_order(1)]

    def gather_copy(direction, n):
        hop, part = orders[direction][n]
        rows = lambda p: txt.at[pl.ds(p * ROWS + part * CHUNK, CHUNK)]
        src = text.at[0, pl.ds(part * CHUNK, CHUNK)] if hop == 1 else rows(place(direction, hop - 1))
        return copy_to(
            src, rows(place(direction, hop)), ag_s.at[direction, n], ag_r.at[direction, n], grp=side[direction]
        )

    def col_copy(direction, hop):
        return copy_to(
            col.at[place(direction, hop - 1)], col.at[place(direction, hop)],
            co_s.at[direction, hop - 1], co_r.at[direction, hop - 1], grp=side[direction],
        )

    gather = [[gather_copy(d, n) for n in range(len(orders[d]))] for d in range(2)]
    cols = [[col_copy(0, hop) for hop in (1, 2, 3, 4)], [col_copy(1, hop) for hop in (1, 2, 3)]]

    def arrived(*steps):
        for n in steps:
            hop = n // PARTS + 1
            for d in range(2):
                gather[d][n].wait_recv()
                if n + PARTS < len(orders[d]):
                    go(gather[d][n + PARTS])
            for d in range(2):
                if n % PARTS == (2 if hop < 4 else 0) and hop <= len(cols[d]):
                    cols[d][hop - 1].wait_recv()
                    if hop < len(cols[d]):
                        go(cols[d][hop])

    def image_copies(src, dst, sem, **to):
        def copy(i):
            start = i * HALF
            rows = image.at[0, pl.ds(start, HALF)] if src == 0 else img.at[pl.ds(src * ROWS + start, HALF)]
            r_sem = im_r.at[2 * (dst - 1) + i]
            return copy_to(rows, img.at[pl.ds(dst * ROWS + start, HALF)], im_s.at[2 * sem + i], r_sem, **to)

        return copy(0), copy(1), copy_to(meta.at[src], meta.at[dst], me_s.at[sem], me_r.at[dst - 1], **to)

    swap = last.astype(jnp.int32)
    z_img = image_copies(0, 1, 0, grp=zpart)
    next_own = image_copies(0, 2 + swap, 1, grp=next_grp, blk=nxt)
    next_other = image_copies(1, 3 - swap, 2, grp=next_grp, blk=nxt)
    passed = {3: image_copies(3, 2, 3, grp=zpart), 2: image_copies(2, 3, 4, grp=zpart)}
    arrivals = {2: image_copies(0, 2, 0, grp=zpart), 3: image_copies(0, 3, 0, grp=zpart)}

    def image_arrived(slot):
        for copy in arrivals[slot]:
            copy.wait_recv()

    def start_if(condition, copies):
        @pl.when(condition)
        def _():
            for copy in copies:
                copy.start()

    def pass_on(condition, slot):
        @pl.when(condition)
        def _():
            for got, copy in zip(arrivals[slot], passed[slot]):
                got.wait_recv()
                copy.start()

    def take(ref, parts):
        pieces = []
        for p, part in parts:
            lo = p * ROWS + part * CHUNK
            if pieces and pieces[-1][1] == lo:
                pieces[-1][1] = lo + CHUNK
            else:
                pieces.append([lo, lo + CHUNK])
        pieces = [ref[lo:hi, :] for lo, hi in pieces]
        return pieces[0] if len(pieces) == 1 else jnp.concatenate(pieces, axis=0)

    def whole(*places):
        return [(p, part) for p in places for part in range(PARTS)]

    def columns(*places):
        for p in places:
            lct[p * ROWS : (p + 1) * ROWS, :] = jnp.broadcast_to(col[p, 0:1, :], (ROWS, ROWS)).T

    def scores(parts, k):
        s = lax.dot_general(
            take(txt, parts), img[k * 2 * ROWS : (k + 1) * 2 * ROWS, :], (((1,), (1,)), ((), ())),
            preferred_element_type=F32,
        )
        s = s * scale
        lr = jnp.concatenate([meta[2 * k, 0:1, :], meta[2 * k + 1, 0:1, :]], axis=1)
        lc = take(lct, parts)
        d = 0.5 * (jnp.exp(s - lr) + jnp.exp(s - jnp.concatenate([lc, lc], axis=1)))
        if k == 0:
            pr = jnp.concatenate([meta[0, 1:2, :], meta[1, 1:2, :]], axis=1).astype(jnp.int32)
            iota = lax.broadcasted_iota(jnp.int32, (CHUNK, 2 * ROWS), 0)
        for i, (p, part) in enumerate(parts):
            rows = d[i * CHUNK : (i + 1) * CHUNK]
            if k == 0:
                rel = 0 if p == 0 else 4 if p == 7 else (RING - (p + 1) // 2) if p % 2 else p // 2
                rows = rows - (pr - (ring[rel] * ROWS + part * CHUNK) == iota).astype(F32)
            lo = p * ROWS + part * CHUNK
            dt[lo : lo + CHUNK, k * 2 * ROWS : (k + 1) * 2 * ROWS] = rows.astype(BF16)

    def contribution(parts):
        c = jnp.dot(take(dt, parts), img[...], preferred_element_type=F32)
        for i, (p, part) in enumerate(parts):
            lo = p * ROWS + part * CHUNK
            ct[lo : lo + CHUNK, :] = c[i * CHUNK : (i + 1) * CHUNK]

    def image_term(k):
        return lax.dot_general(
            dt[:, k * 2 * ROWS : (k + 1) * 2 * ROWS], txt[...], (((0,), (0,)), ((), ())), preferred_element_type=F32
        )

    r_orders = [reduce_order(0), reduce_order(1)]

    def reduce_copy(direction, n):
        rows = pl.ds(n * CHUNK, CHUNK)
        return copy_to(
            rsend.at[direction, rows], rrecv.at[direction, rows],
            rs_s.at[direction, n], rs_r.at[direction, n], grp=side[direction],
        )

    reduction = [[reduce_copy(d, n) for n in range(len(r_orders[d]))] for d in range(2)]

    def reduce_step(*steps):
        for n in steps:
            for d in range(2):
                hops, part = r_orders[d][n]
                start = place(1 - d, hops) * ROWS + part * CHUNK
                total = ct[start : start + CHUNK, :]
                if (hops + 1, part) in r_orders[d]:
                    m = r_orders[d].index((hops + 1, part))
                    reduction[d][m].wait_recv()
                    total = total + rrecv[d, m * CHUNK : (m + 1) * CHUNK, :].astype(F32)
                rsend[d, n * CHUNK : (n + 1) * CHUNK, :] = total.astype(BF16)
                go(reduction[d][n])

    half = lambda j: slice(j * HALF, (j + 1) * HALF)
    feeder = jnp.logical_and(first, z_lo == 1)
    back_blk = jnp.where(feeder, b, prv)

    def back_copy(j):
        if j < 2:
            to = jnp.where(feeder, j + 6, jnp.where(inlet, j + 2, j))
        else:
            to = jnp.where(feeder, j + 2, jnp.where(inlet, j - 2, j))
        return copy_to(
            gis.at[pl.ds(j * HALF, HALF)], gir.at[pl.ds(pl.multiple_of(to * HALF, HALF), HALF)],
            gi_s.at[j], gi_r.at[to], grp=prev_grp, blk=back_blk,
        )

    back = [back_copy(j) for j in range(4)]

    def back_wait(to):
        rows = pl.ds(to * HALF, HALF)
        copy_to(gis.at[pl.ds(0, HALF)], gir.at[rows], gi_s.at[0], gi_r.at[to], grp=zpart).wait_recv()

    def inlet_back(j):
        @pl.when(inlet)
        def _():
            back_wait(4 + j)
            gis[half(j), :] = (g1[half(j), :] + gir[half(4 + j), :].astype(F32)).astype(BF16)
            back[j].start()

    z_own = [
        copy_to(zs.at[pl.ds(i * HALF, HALF)], zr.at[pl.ds(i * HALF, HALF)], zz_s.at[i], zz_r.at[i], grp=zpart)
        for i in range(2)
    ]

    def own_back(condition):
        @pl.when(condition)
        def _():
            for i in range(2):

                @pl.when(has_next)
                def _():
                    back_wait(2 + i)

                zs[half(i), :] = (g0[half(2 + i), :] + gir[half(2 + i), :].astype(F32)).astype(BF16)
                z_own[i].start()

    pl.semaphore_wait(barrier, 3 + has_next.astype(jnp.int32))
    for n in range(PARTS):
        for d in range(2):
            go(gather[d][n])
    start_if(True, z_img[:2])
    start_if(has_next, next_own[:2])
    for copy in local[:3]:
        copy.wait()
    meta[0] = jnp.zeros((8, ROWS), F32)
    meta[0, 0:1, :] = vecs[0].astype(F32)
    meta[0, 1:2, :] = pairs[...].astype(F32)
    col[0] = jnp.broadcast_to(vecs[1].astype(F32), (8, ROWS))
    start_if(True, z_img[2:])
    start_if(has_next, next_own[2:])
    for d in range(2):
        go(cols[d][0])
    for copy in local[3:]:
        copy.wait()
    columns(0)
    arrived(0, 1)

    @pl.when(outlet)
    def _():
        for got, copy in zip(z_img, next_other):
            got.wait_recv()
            copy.start()

    arrived(2)
    pass_on(jnp.logical_and(inlet, jnp.logical_not(zero)), 3)
    arrived(3)

    @pl.when(jnp.logical_not(outlet))
    def _():
        for copy in z_img:
            copy.wait_recv()

    start_if(jnp.logical_not(last), next_other)
    columns(1, 2)
    scores(whole(0), 0)
    arrived(4)
    pass_on(jnp.logical_and(inlet, jnp.logical_not(zero)), 2)
    scores(whole(1, 2), 0)
    arrived(5, 6, 7)
    pass_on(jnp.logical_and(inlet, zero), 3)
    columns(3, 4)
    scores(whole(3, 4), 0)
    arrived(8, 9)
    pass_on(jnp.logical_and(inlet, zero), 2)
    near = [(5, part) for part in FAR[0]] + [(6, part) for part in FAR[1]]
    far = [(5, part) for part in FAR[1]] + [(6, part) for part in FAR[0]]
    arrived(10)
    columns(5, 6)
    scores(near, 0)

    @pl.when(jnp.logical_not(inlet))
    def _():
        image_arrived(2)
        image_arrived(3)

    scores(near, 1)
    contribution(near)
    reduce_step(0, 1)
    scores(whole(0), 1)
    scores(whole(1, 2), 1)
    arrived(11)
    scores(whole(3, 4), 1)
    scores(far, 0)
    scores(far, 1)
    arrived(12)
    columns(7)
    opposite = sorted([(7, FAR[0][0]), (7, FAR[1][0])])
    scores(opposite, 0)
    scores(opposite, 1)
    contribution(opposite)
    reduce_step(2)
    arrived(13)
    opposite = sorted([(7, FAR[0][1]), (7, FAR[1][1])])
    scores(opposite, 0)
    scores(opposite, 1)
    contribution(opposite)
    reduce_step(3)
    g1[...] = image_term(1)

    @pl.when(jnp.logical_not(inlet))
    def _():
        for j in (2, 3, 0, 1):
            gis[half(j), :] = g1[half(j), :].astype(BF16)
            back[j].start()

    @pl.when(jnp.logical_not(has_next))
    def _():
        gir[0 : 2 * ROWS, :] = jnp.zeros((2 * ROWS, gir.shape[1]), BF16)

    contribution(whole(3, 4))
    reduce_step(4)
    contribution(far)
    reduce_step(5, 6)
    contribution(whole(1, 2))
    g0[...] = image_term(0)
    contribution(whole(0))
    reduce_step(7, 8)
    own_back(jnp.logical_not(last))
    inlet_back(0)
    reduce_step(9)
    inlet_back(1)
    reduce_step(10)
    inlet_back(2)
    reduce_step(11)
    inlet_back(3)
    reduce_step(12, 13)
    own_back(last)

    @pl.when(has_next)
    def _():
        back_wait(0)
        back_wait(1)

    for copy in z_own:
        copy.wait_recv()
    oi[...] = (scale * (g0[:ROWS, :] + gir[:ROWS, :].astype(F32) + zr[...].astype(F32))).astype(BF16)
    outs = [pltpu.make_async_copy(oi, gi_out.at[0], out_sem.at[0])]
    outs[0].start()
    for part in sorted(range(PARTS), key=lambda part: r_orders[0].index((1, part)) + r_orders[1].index((1, part))):
        rows = pl.ds(part * CHUNK, CHUNK)
        total = ct[part * CHUNK : (part + 1) * CHUNK, :]
        for d in range(2):
            m = r_orders[d].index((1, part))
            reduction[d][m].wait_recv()
            total = total + rrecv[d, m * CHUNK : (m + 1) * CHUNK, :].astype(F32)
        ot[part * CHUNK : (part + 1) * CHUNK, :] = (scale * total).astype(BF16)
        outs.append(pltpu.make_async_copy(ot.at[rows], gt_out.at[0, rows], out_sem.at[1 + part]))
        outs[-1].start()
    for copy in started:
        copy.wait_send()
    for copy in (*z_img, *back, *z_own):
        copy.wait_send()

    @pl.when(has_next)
    def _():
        for copy in next_own + next_other:
            copy.wait_send()

    @pl.when(inlet)
    def _():
        for copy in passed[2] + passed[3]:
            copy.wait_send()

    for copy in outs:
        copy.wait()


def body(image, text, logit_scale, lse_row, lse_col, pair):
    width = image.shape[2]
    msgs = 3 * PARTS + PARTS // 2
    hbm = pl.BlockSpec(memory_space=pltpu.HBM)
    dma = pltpu.SemaphoreType.DMA
    out = jax.ShapeDtypeStruct((1, ROWS, width), BF16)
    return pl.pallas_call(
        kernel,
        out_shape=(out, out),
        in_specs=[hbm, hbm, pl.BlockSpec(memory_space=pltpu.SMEM), hbm, hbm, hbm],
        out_specs=(hbm, hbm),
        scratch_shapes=[
            pltpu.VMEM((PLACES * ROWS, width), BF16),
            pltpu.VMEM((4 * ROWS, width), BF16),
            pltpu.VMEM((4, 8, ROWS), F32),
            pltpu.VMEM((PLACES, 8, ROWS), F32),
            pltpu.VMEM((PLACES * ROWS, ROWS), F32),
            pltpu.VMEM((PLACES * ROWS, 4 * ROWS), BF16),
            pltpu.VMEM((PLACES * ROWS, width), F32),
            pltpu.VMEM((2, msgs * CHUNK, width), BF16),
            pltpu.VMEM((2, msgs * CHUNK, width), BF16),
            pltpu.VMEM((2 * ROWS, width), F32),
            pltpu.VMEM((2 * ROWS, width), F32),
            pltpu.VMEM((2 * ROWS, width), BF16),
            pltpu.VMEM((4 * ROWS, width), BF16),
            pltpu.VMEM((ROWS, width), BF16),
            pltpu.VMEM((ROWS, width), BF16),
            pltpu.VMEM((2, 1, ROWS), BF16),
            pltpu.VMEM((1, ROWS), jnp.int32),
            pltpu.VMEM((ROWS, width), BF16),
            pltpu.VMEM((ROWS, width), BF16),
            dma((5,)),
            dma((1 + PARTS,)),
            dma((2, msgs)),
            dma((2, msgs)),
            dma((2, msgs)),
            dma((2, msgs)),
            dma((10,)),
            dma((6,)),
            dma((5,)),
            dma((3,)),
            dma((2, 4)),
            dma((2, 4)),
            dma((4,)),
            dma((8,)),
            dma((2,)),
            dma((2,)),
        ],
        compiler_params=pltpu.CompilerParams(
            collective_id=0, has_side_effects=True, vmem_limit_bytes=63 * 2**20
        ),
        cost_estimate=pl.CostEstimate(
            flops=12 * ROWS * 16 * ROWS * width, bytes_accessed=8 * ROWS * width, transcendentals=8 * ROWS * 16 * ROWS
        ),
    )(image, text, jnp.reshape(logit_scale, (1,)), lse_row, lse_col, pair)


def solution(mesh):
    return jax.shard_map(
        body,
        mesh=mesh,
        in_specs=(
            P("blk", "grp", None),
            P("blk", "grp", None),
            P(),
            P("blk", "grp"),
            P("blk", "grp"),
            P("blk", "grp"),
        ),
        out_specs=(P("blk", "grp", None), P("blk", "grp", None)),
        check_vma=False,
    )
```

time: 341 us -> 56.1 us (0.16)
  the two profiles are of different devices: /device:TPU:6 before, /device:TPU:64 now
where the time goes in v2:
time: 56.1 us; the launch traced here: 56 us
  Pallas kernels  52.2 us (93%)
  local copies, waits for them, and re-layouts  2.42 us (4%)
  between operations  1.29 us (2%)
    pallas_call x1, Pallas kernels, body(): pl.pallas_call(kernel, out_shape=(out, out), in_specs=[hbm, hbm, pl.Block...  52.2 us
    unnamed x4, local copies, waits for them, and re-layouts  2.42 us

profile of v2, /device:TPU:64, one launch (start us, length us, event | category | flops | bytes accessed | tf_op | source)
XLA Modules:
  0.0 56.0 jit_solution(13358793766117783648)
XLA Ops:
  1.3 52.2 %shard_map.77 = (bf16[1,128,1024]{2,1,0:T(8,128)(2,1)}, bf16[1,128,1024]{2,1,0:T(8,128)(2,1)}) custom-call(bf16[1,128,1024]{2,1,0:T(8,128)(2,1)} %image.1, bf16[1,128,1024]{2,1,0:T(8,128)(2,1)} %text.1, f32[1]{0:T(128)} %bitcast.1.scale_ref, bf16[1,128]{1,0:T(2,128)(2,1)} %lrow_ref.1, bf16[1,128]{1,0:T(2,128)(2,1)} %lcol_ref.1, s32[1,128]{1,0:T(1,128)} %pair_ref.1), custom_call_target="tpu_custom_call" | custom-call | flops 3221225472 | bytes 1048576 | tf_op jit(solution)/shard_map/pallas_call | solution.py:445
  53.5 0.0 copy-start
  53.5 1.7 %copy.11 = bf16[1,128,1024]{2,1,0:T(8,128)(2,1)} copy(bf16[1,128,1024]{2,1,0:T(8,128)(2,1)} %get-tuple-element.4) | data formatting | bytes 524288
  55.2 0.0 copy-done
  55.2 0.7 %copy.12 = bf16[1,128,1024]{2,1,0:T(8,128)(2,1)} copy(bf16[1,128,1024]{2,1,0:T(8,128)(2,1)S(1)} %copy-done) | data formatting | bytes 524288
Async XLA Ops:
  53.5 1.7 %copy-start = (bf16[1,128,1024]{2,1,0:T(8,128)(2,1)S(1)}, bf16[1,128,1024]{2,1,0:T(8,128)(2,1)}, u32[]{:S(2)}) copy-start(bf16[1,128,1024]{2,1,0:T(8,128)(2,1)} %get-tuple-element.5) | copy-start | bytes 786436

commit v3 on v2

--- a/solution.py
+++ b/solution.py
@@ -11,6 +11,7 @@
 RING = 8
 ROWS = 128
 PARTS = 4
+STEP = PARTS // 4
 CHUNK = ROWS // PARTS
 HALF = ROWS // 2
 PLACES = 8
@@ -31,18 +32,19 @@
 
 
 def reduce_order(direction):
-    f0, f1 = FAR[direction]
-    n0, n1 = FAR[1 - direction]
-    return [
+    f0, f1 = FAR[direction][:STEP], FAR[direction][STEP:]
+    n0, n1 = FAR[1 - direction][:STEP], FAR[1 - direction][STEP:]
+    order = [
         (3, n0), (3, n1), (4, f0), (4, f1), (2, n0), (3, f0), (3, f1),
         (2, n1), (2, f0), (2, f1), (1, n0), (1, f0), (1, f1), (1, n1),
     ]
+    return [(hops, part) for hops, parts in order for part in parts]
 
 
 def kernel(
     image, text, scale_ref, lrow_ref, lcol_ref, pair_ref, gi_out, gt_out,
-    txt, img, meta, col, lct, dt, ct, rsend, rrecv, g0, g1, gis, gir, zs, zr, vecs, pairs, oi, ot,
-    local_sem, out_sem, ag_s, ag_r, rs_s, rs_r, im_s, im_r, me_s, me_r, co_s, co_r, gi_s, gi_r, zz_s, zz_r,
+    txt, img, imgt, meta, col, lct, dt, ct, rsend, rrecv, g0, g1, gis, gir, zs, zr, vecs, pairs,
+    local_sem, ag_s, rs_s, ring_r, im_s, im_r, me_s, me_r, co_s, co_r, gi_s, gi_r, zz_s, zz_r,
 ):
     g = lax.axis_index("grp")
     b = lax.axis_index("blk")
@@ -96,12 +98,9 @@
     for copy in local:
         copy.start()
     scale = scale_ref[0]
-    started = []
 
     def go(copy):
         copy.start()
-        started.append(copy)
-        return copy
 
     orders = [gather_order(0), gather_order(1)]
 
@@ -110,27 +109,27 @@
         rows = lambda p: txt.at[pl.ds(p * ROWS + part * CHUNK, CHUNK)]
         src = text.at[0, pl.ds(part * CHUNK, CHUNK)] if hop == 1 else rows(place(direction, hop - 1))
         return copy_to(
-            src, rows(place(direction, hop)), ag_s.at[direction, n], ag_r.at[direction, n], grp=side[direction]
+            src, rows(place(direction, hop)), ag_s, ring_r.at[direction, n], grp=side[direction]
         )
 
     def col_copy(direction, hop):
         return copy_to(
             col.at[place(direction, hop - 1)], col.at[place(direction, hop)],
-            co_s.at[direction, hop - 1], co_r.at[direction, hop - 1], grp=side[direction],
+            co_s, co_r.at[direction, hop - 1], grp=side[direction],
         )
 
     gather = [[gather_copy(d, n) for n in range(len(orders[d]))] for d in range(2)]
     cols = [[col_copy(0, hop) for hop in (1, 2, 3, 4)], [col_copy(1, hop) for hop in (1, 2, 3)]]
 
     def arrived(*steps):
-        for n in steps:
+        for n in [STEP * step + i for step in steps for i in range(STEP)]:
             hop = n // PARTS + 1
             for d in range(2):
                 gather[d][n].wait_recv()
                 if n + PARTS < len(orders[d]):
                     go(gather[d][n + PARTS])
             for d in range(2):
-                if n % PARTS == (2 if hop < 4 else 0) and hop <= len(cols[d]):
+                if n % PARTS == (PARTS // 2 if hop < 4 else 0) and hop <= len(cols[d]):
                     cols[d][hop - 1].wait_recv()
                     if hop < len(cols[d]):
                         go(cols[d][hop])
@@ -140,7 +139,7 @@
             start = i * HALF
             rows = image.at[0, pl.ds(start, HALF)] if src == 0 else img.at[pl.ds(src * ROWS + start, HALF)]
             r_sem = im_r.at[2 * (dst - 1) + i]
-            return copy_to(rows, img.at[pl.ds(dst * ROWS + start, HALF)], im_s.at[2 * sem + i], r_sem, **to)
+            return copy_to(rows, img.at[pl.ds(dst * ROWS + start, HALF)], im_s.at[sem], r_sem, **to)
 
         return copy(0), copy(1), copy_to(meta.at[src], meta.at[dst], me_s.at[sem], me_r.at[dst - 1], **to)
 
@@ -186,25 +185,23 @@
         for p in places:
             lct[p * ROWS : (p + 1) * ROWS, :] = jnp.broadcast_to(col[p, 0:1, :], (ROWS, ROWS)).T
 
-    def scores(parts, k):
-        s = lax.dot_general(
-            take(txt, parts), img[k * 2 * ROWS : (k + 1) * 2 * ROWS, :], (((1,), (1,)), ((), ())),
-            preferred_element_type=F32,
-        )
-        s = s * scale
-        lr = jnp.concatenate([meta[2 * k, 0:1, :], meta[2 * k + 1, 0:1, :]], axis=1)
+    def turn(slot):
+        imgt[:, slot * ROWS : (slot + 1) * ROWS] = img[slot * ROWS : (slot + 1) * ROWS, :].T
+
+    def scores(parts):
+        s = jnp.dot(take(txt, parts), imgt[...], preferred_element_type=F32) * scale
+        lr = jnp.concatenate([meta[slot, 0:1, :] for slot in range(4)], axis=1)
         lc = take(lct, parts)
-        d = 0.5 * (jnp.exp(s - lr) + jnp.exp(s - jnp.concatenate([lc, lc], axis=1)))
-        if k == 0:
-            pr = jnp.concatenate([meta[0, 1:2, :], meta[1, 1:2, :]], axis=1).astype(jnp.int32)
-            iota = lax.broadcasted_iota(jnp.int32, (CHUNK, 2 * ROWS), 0)
+        d = 0.5 * (jnp.exp(s - lr) + jnp.exp(s - jnp.concatenate([lc] * 4, axis=1)))
+        pr = jnp.concatenate([meta[0, 1:2, :], meta[1, 1:2, :]], axis=1).astype(jnp.int32)
+        iota = lax.broadcasted_iota(jnp.int32, (CHUNK, 2 * ROWS), 0)
         for i, (p, part) in enumerate(parts):
+            rel = 0 if p == 0 else 4 if p == 7 else (RING - (p + 1) // 2) if p % 2 else p // 2
             rows = d[i * CHUNK : (i + 1) * CHUNK]
-            if k == 0:
-                rel = 0 if p == 0 else 4 if p == 7 else (RING - (p + 1) // 2) if p % 2 else p // 2
-                rows = rows - (pr - (ring[rel] * ROWS + part * CHUNK) == iota).astype(F32)
+            own = rows[:, : 2 * ROWS] - (pr - (ring[rel] * ROWS + part * CHUNK) == iota).astype(F32)
             lo = p * ROWS + part * CHUNK
-            dt[lo : lo + CHUNK, k * 2 * ROWS : (k + 1) * 2 * ROWS] = rows.astype(BF16)
+            dt[lo : lo + CHUNK, : 2 * ROWS] = own.astype(BF16)
+            dt[lo : lo + CHUNK, 2 * ROWS :] = rows[:, 2 * ROWS :].astype(BF16)
 
     def contribution(parts):
         c = jnp.dot(take(dt, parts), img[...], preferred_element_type=F32)
@@ -223,13 +220,13 @@
         rows = pl.ds(n * CHUNK, CHUNK)
         return copy_to(
             rsend.at[direction, rows], rrecv.at[direction, rows],
-            rs_s.at[direction, n], rs_r.at[direction, n], grp=side[direction],
+            rs_s, ring_r.at[direction, n], grp=side[direction],
         )
 
     reduction = [[reduce_copy(d, n) for n in range(len(r_orders[d]))] for d in range(2)]
 
     def reduce_step(*steps):
-        for n in steps:
+        for n in [STEP * step + i for step in steps for i in range(STEP)]:
             for d in range(2):
                 hops, part = r_orders[d][n]
                 start = place(1 - d, hops) * ROWS + part * CHUNK
@@ -252,14 +249,14 @@
             to = jnp.where(feeder, j + 2, jnp.where(inlet, j - 2, j))
         return copy_to(
             gis.at[pl.ds(j * HALF, HALF)], gir.at[pl.ds(pl.multiple_of(to * HALF, HALF), HALF)],
-            gi_s.at[j], gi_r.at[to], grp=prev_grp, blk=back_blk,
+            gi_s, gi_r.at[to], grp=prev_grp, blk=back_blk,
         )
 
     back = [back_copy(j) for j in range(4)]
 
     def back_wait(to):
         rows = pl.ds(to * HALF, HALF)
-        copy_to(gis.at[pl.ds(0, HALF)], gir.at[rows], gi_s.at[0], gi_r.at[to], grp=zpart).wait_recv()
+        copy_to(gis.at[pl.ds(0, HALF)], gir.at[rows], gi_s, gi_r.at[to], grp=zpart).wait_recv()
 
     def inlet_back(j):
         @pl.when(inlet)
@@ -269,7 +266,7 @@
             back[j].start()
 
     z_own = [
-        copy_to(zs.at[pl.ds(i * HALF, HALF)], zr.at[pl.ds(i * HALF, HALF)], zz_s.at[i], zz_r.at[i], grp=zpart)
+        copy_to(zs.at[pl.ds(i * HALF, HALF)], zr.at[pl.ds(i * HALF, HALF)], zz_s, zz_r.at[i], grp=zpart)
         for i in range(2)
     ]
 
@@ -322,48 +319,43 @@
             copy.wait_recv()
 
     start_if(jnp.logical_not(last), next_other)
+    turn(0)
+    turn(1)
     columns(1, 2)
-    scores(whole(0), 0)
     arrived(4)
     pass_on(jnp.logical_and(inlet, jnp.logical_not(zero)), 2)
-    scores(whole(1, 2), 0)
     arrived(5, 6, 7)
     pass_on(jnp.logical_and(inlet, zero), 3)
     columns(3, 4)
-    scores(whole(3, 4), 0)
     arrived(8, 9)
     pass_on(jnp.logical_and(inlet, zero), 2)
-    near = [(5, part) for part in FAR[0]] + [(6, part) for part in FAR[1]]
-    far = [(5, part) for part in FAR[1]] + [(6, part) for part in FAR[0]]
+    near = sorted([(5, part) for part in FAR[0]] + [(6, part) for part in FAR[1]])
+    far = sorted([(5, part) for part in FAR[1]] + [(6, part) for part in FAR[0]])
+
+    @pl.when(jnp.logical_not(inlet))
+    def _():
+        image_arrived(2)
+        image_arrived(3)
+
+    turn(2)
+    turn(3)
     arrived(10)
     columns(5, 6)
-    scores(near, 0)
-
-    @pl.when(jnp.logical_not(inlet))
-    def _():
-        image_arrived(2)
-        image_arrived(3)
-
-    scores(near, 1)
+    scores(near)
     contribution(near)
     reduce_step(0, 1)
-    scores(whole(0), 1)
-    scores(whole(1, 2), 1)
+    scores(whole(0, 1, 2, 3, 4))
     arrived(11)
-    scores(whole(3, 4), 1)
-    scores(far, 0)
-    scores(far, 1)
+    scores(far)
     arrived(12)
     columns(7)
-    opposite = sorted([(7, FAR[0][0]), (7, FAR[1][0])])
-    scores(opposite, 0)
-    scores(opposite, 1)
+    opposite = sorted((7, part) for d in range(2) for part in FAR[d][:STEP])
+    scores(opposite)
     contribution(opposite)
     reduce_step(2)
     arrived(13)
-    opposite = sorted([(7, FAR[0][1]), (7, FAR[1][1])])
-    scores(opposite, 0)
-    scores(opposite, 1)
+    opposite = sorted((7, part) for d in range(2) for part in FAR[d][STEP:])
+    scores(opposite)
     contribution(opposite)
     reduce_step(3)
     g1[...] = image_term(1)
@@ -404,35 +396,44 @@
 
     for copy in z_own:
         copy.wait_recv()
-    oi[...] = (scale * (g0[:ROWS, :] + gir[:ROWS, :].astype(F32) + zr[...].astype(F32))).astype(BF16)
-    outs = [pltpu.make_async_copy(oi, gi_out.at[0], out_sem.at[0])]
-    outs[0].start()
+    gi_out[0] = (scale * (g0[:ROWS, :] + gir[:ROWS, :].astype(F32) + zr[...].astype(F32))).astype(BF16)
     for part in sorted(range(PARTS), key=lambda part: r_orders[0].index((1, part)) + r_orders[1].index((1, part))):
-        rows = pl.ds(part * CHUNK, CHUNK)
         total = ct[part * CHUNK : (part + 1) * CHUNK, :]
         for d in range(2):
             m = r_orders[d].index((1, part))
             reduction[d][m].wait_recv()
             total = total + rrecv[d, m * CHUNK : (m + 1) * CHUNK, :].astype(F32)
-        ot[part * CHUNK : (part + 1) * CHUNK, :] = (scale * total).astype(BF16)
-        outs.append(pltpu.make_async_copy(ot.at[rows], gt_out.at[0, rows], out_sem.at[1 + part]))
-        outs[-1].start()
-    for copy in started:
-        copy.wait_send()
-    for copy in (*z_img, *back, *z_own):
-        copy.wait_send()
+        gt_out[0, part * CHUNK : (part + 1) * CHUNK, :] = (scale * total).astype(BF16)
+
+    def all_sent(ref, sem):
+        pltpu.make_async_copy(ref, ref, sem).wait()
+
+    def images_sent(*sems):
+        for sem in sems:
+            all_sent(img.at[pl.ds(0, ROWS)], im_s.at[sem])
+            all_sent(meta.at[0], me_s.at[sem])
+
+    all_sent(rrecv, ag_s)
+    all_sent(rrecv, rs_s)
+    all_sent(col.at[pl.ds(0, 7)], co_s)
+    all_sent(gis, gi_s)
+    all_sent(zs, zz_s)
+    images_sent(0)
 
     @pl.when(has_next)
     def _():
-        for copy in next_own + next_other:
-            copy.wait_send()
+        images_sent(1, 2)
 
     @pl.when(inlet)
     def _():
-        for copy in passed[2] + passed[3]:
-            copy.wait_send()
-
-    for copy in outs:
+        images_sent(3, 4)
+
+
+def write(gi, gt, gi_out, gt_out, sems):
+    copies = [pltpu.make_async_copy(src, dst, sems.at[i]) for i, (src, dst) in enumerate(((gi, gi_out), (gt, gt_out)))]
+    for copy in copies:
+        copy.start()
+    for copy in copies:
         copy.wait()
 
 
@@ -441,15 +442,17 @@
     msgs = 3 * PARTS + PARTS // 2
     hbm = pl.BlockSpec(memory_space=pltpu.HBM)
     dma = pltpu.SemaphoreType.DMA
-    out = jax.ShapeDtypeStruct((1, ROWS, width), BF16)
-    return pl.pallas_call(
+    vmem = pl.BlockSpec(memory_space=pltpu.VMEM)
+    out = pltpu.VMEM((1, ROWS, width), BF16)
+    grads = pl.pallas_call(
         kernel,
         out_shape=(out, out),
         in_specs=[hbm, hbm, pl.BlockSpec(memory_space=pltpu.SMEM), hbm, hbm, hbm],
-        out_specs=(hbm, hbm),
+        out_specs=(vmem, vmem),
         scratch_shapes=[
             pltpu.VMEM((PLACES * ROWS, width), BF16),
             pltpu.VMEM((4 * ROWS, width), BF16),
+            pltpu.VMEM((width, 4 * ROWS), BF16),
             pltpu.VMEM((4, 8, ROWS), F32),
             pltpu.VMEM((PLACES, 8, ROWS), F32),
             pltpu.VMEM((PLACES * ROWS, ROWS), F32),
@@ -465,23 +468,19 @@
             pltpu.VMEM((ROWS, width), BF16),
             pltpu.VMEM((2, 1, ROWS), BF16),
             pltpu.VMEM((1, ROWS), jnp.int32),
-            pltpu.VMEM((ROWS, width), BF16),
-            pltpu.VMEM((ROWS, width), BF16),
             dma((5,)),
-            dma((1 + PARTS,)),
+            dma,
+            dma,
             dma((2, msgs)),
-            dma((2, msgs)),
-            dma((2, msgs)),
-            dma((2, msgs)),
-            dma((10,)),
+            dma((5,)),
             dma((6,)),
             dma((5,)),
             dma((3,)),
+            dma,
             dma((2, 4)),
-            dma((2, 4)),
-            dma((4,)),
+            dma,
             dma((8,)),
-            dma((2,)),
+            dma,
             dma((2,)),
         ],
         compiler_params=pltpu.CompilerParams(
@@ -491,6 +490,14 @@
             flops=12 * ROWS * 16 * ROWS * width, bytes_accessed=8 * ROWS * width, transcendentals=8 * ROWS * 16 * ROWS
         ),
     )(image, text, jnp.reshape(logit_scale, (1,)), lse_row, lse_col, pair)
+    return pl.pallas_call(
+        write,
+        out_shape=[jax.ShapeDtypeStruct((1, ROWS, width), BF16)] * 2,
+        in_specs=[vmem, vmem],
+        out_specs=[hbm, hbm],
+        scratch_shapes=[dma((2,))],
+        compiler_params=pltpu.CompilerParams(vmem_limit_bytes=2**20),
+    )(*grads)
 
 
 def solution(mesh):

time: 56.1 us -> 52.9 us (0.943)
  local copies, waits for them, and re-layouts: 2.42 us -> 0 us
  Pallas kernels: 52.2 us -> 51.4 us
    unnamed x4 -> x0, local copies, waits for them, and re-layouts: 2.42 us -> none
    pallas_call x1, Pallas kernels: 52.2 us -> 50.6 us  [body(): pl.pallas_call(kernel, out_shape=(out, out), in_specs=[hbm, hbm, pl.Block...]
    pallas_call x0 -> x1, Pallas kernels: none -> 0.81 us  [body(): pl.pallas_call(write, out_shape=[jax.ShapeDtypeStruct((1, ROWS, width), B...]
where the time goes in v3:
time: 52.9 us; the launch traced here: 52.7 us
  Pallas kernels  51.4 us (97%)
  between operations  1.28 us (2%)
    pallas_call x1, Pallas kernels, body(): pl.pallas_call(kernel, out_shape=(out, out), in_specs=[hbm, hbm, pl.Block...  50.6 us

profile of v3, /device:TPU:64, one launch (start us, length us, event | category | flops | bytes accessed | tf_op | source)
XLA Modules:
  0.0 52.7 jit_solution(11672587845186287908)
XLA Ops:
  1.3 50.6 %shard_map.77 = (bf16[1,128,1024]{2,1,0:T(8,128)(2,1)S(1)}, bf16[1,128,1024]{2,1,0:T(8,128)(2,1)S(1)}) custom-call(bf16[1,128,1024]{2,1,0:T(8,128)(2,1)} %image.1, bf16[1,128,1024]{2,1,0:T(8,128)(2,1)} %text.1, f32[1]{0:T(128)} %bitcast.1.scale_ref, bf16[1,128]{1,0:T(2,128)(2,1)} %lrow_ref.1, bf16[1,128]{1,0:T(2,128)(2,1)} %lcol_ref.1, s32[1,128]{1,0:T(1,128)} %pair_ref.1), custom_call_target="tpu_custom_call" | custom-call | flops 3221225472 | bytes 1048576 | tf_op jit(solution)/shard_map/pallas_call | solution.py:447
  51.9 0.8 %shard_map.78 = (bf16[1,128,1024]{2,1,0:T(8,128)(2,1)}, bf16[1,128,1024]{2,1,0:T(8,128)(2,1)}) custom-call(bf16[1,128,1024]{2,1,0:T(8,128)(2,1)S(1)} %get-tuple-element.4.gi, bf16[1,128,1024]{2,1,0:T(8,128)(2,1)S(1)} %get-tuple-element.5.gt), custom_call_target="tpu_custom_call" | custom-call | tf_op jit(solution)/shard_map/pallas_call | solution.py:493

commit v4 on v3

--- a/solution.py
+++ b/solution.py
@@ -44,7 +44,7 @@
 def kernel(
     image, text, scale_ref, lrow_ref, lcol_ref, pair_ref, gi_out, gt_out,
     txt, img, imgt, meta, col, lct, dt, ct, rsend, rrecv, g0, g1, gis, gir, zs, zr, vecs, pairs,
-    local_sem, ag_s, rs_s, ring_r, im_s, im_r, me_s, me_r, co_s, co_r, gi_s, gi_r, zz_s, zz_r,
+    ready, local_sem, ag_s, rs_s, ring_r, im_s, im_r, me_s, me_r, co_s, co_r, gi_s, gi_r, zz_s, zz_r,
 ):
     g = lax.axis_index("grp")
     b = lax.axis_index("blk")
@@ -59,25 +59,40 @@
     last = lax.rem(b, RUN) == RUN - 1
     first = lax.rem(b, RUN) == 0
     zero = b == 0
-    has_next = jnp.logical_not(jnp.logical_and(last, z_lo == 0))
-    has_prev = jnp.logical_not(jnp.logical_and(first, z_lo == 1))
-    outlet = jnp.logical_and(last, z_lo == 1)
-    inlet = jnp.logical_and(first, z_lo == 0)
+    low, high = z_lo == 0, z_lo == 1
+    no = jnp.logical_not
+    both = jnp.logical_and
+    has_next = no(both(last, low))
+    has_prev = no(both(first, high))
+    outlet = both(last, high)
+    inlet = both(first, low)
     next_grp = jnp.where(last, zpart, g)
     prev_grp = jnp.where(first, zpart, g)
 
+    y = g // 2
+    origin = both(zero, low)
+    left_first = jnp.where(y == 0, origin, both(y < 7, no(both(origin, y == 1))))
+    right_first = jnp.where(y == 0, origin, jnp.where(y == 7, no(origin), y == 6))
+    z_first = jnp.where(both(zero, y == 0), low, high)
+    prev_first = both(has_prev, no(zero))
+    next_first = both(has_next, nxt == 0)
+    meets = (
+        (left_first, True, side[1], b, 1),
+        (right_first, True, side[0], b, 0),
+        (z_first, True, zpart, b, 2),
+        (prev_first, has_prev, prev_grp, prv, 3),
+        (next_first, has_next, next_grp, nxt, None),
+    )
     barrier = pltpu.get_barrier_semaphore()
 
-    def greet(grp, blk):
-        pl.semaphore_signal(barrier, inc=1, device_id={"grp": grp, "blk": blk}, device_id_type=MESH)
-
-    greet(side[0], b)
-    greet(side[1], b)
-    greet(zpart, b)
-
-    @pl.when(has_prev)
-    def _():
-        greet(prev_grp, prv)
+    def greet(grp, blk, sem):
+        pl.semaphore_signal(sem, inc=1, device_id={"grp": grp, "blk": blk}, device_id_type=MESH)
+
+    for they_first, met, grp, blk, _ in meets:
+
+        @pl.when(both(met, no(they_first)))
+        def _(grp=grp, blk=blk):
+            greet(grp, blk, barrier)
 
     def copy_to(src, dst, s_sem, r_sem, grp=g, blk=b):
         return pltpu.make_async_remote_copy(
@@ -125,14 +140,13 @@
         for n in [STEP * step + i for step in steps for i in range(STEP)]:
             hop = n // PARTS + 1
             for d in range(2):
+                if n % PARTS == 0 and hop <= len(cols[d]):
+                    cols[d][hop - 1].wait_recv()
+                    if hop < len(cols[d]):
+                        go(cols[d][hop])
                 gather[d][n].wait_recv()
                 if n + PARTS < len(orders[d]):
                     go(gather[d][n + PARTS])
-            for d in range(2):
-                if n % PARTS == (PARTS // 2 if hop < 4 else 0) and hop <= len(cols[d]):
-                    cols[d][hop - 1].wait_recv()
-                    if hop < len(cols[d]):
-                        go(cols[d][hop])
 
     def image_copies(src, dst, sem, **to):
         def copy(i):
@@ -258,8 +272,8 @@
         rows = pl.ds(to * HALF, HALF)
         copy_to(gis.at[pl.ds(0, HALF)], gir.at[rows], gi_s, gi_r.at[to], grp=zpart).wait_recv()
 
-    def inlet_back(j):
-        @pl.when(inlet)
+    def inlet_back(condition, j):
+        @pl.when(both(inlet, condition))
         def _():
             back_wait(4 + j)
             gis[half(j), :] = (g1[half(j), :] + gir[half(4 + j), :].astype(F32)).astype(BF16)
@@ -270,10 +284,10 @@
         for i in range(2)
     ]
 
-    def own_back(condition):
+    def own_back(condition, *halves):
         @pl.when(condition)
         def _():
-            for i in range(2):
+            for i in halves:
 
                 @pl.when(has_next)
                 def _():
@@ -282,53 +296,110 @@
                 zs[half(i), :] = (g0[half(2 + i), :] + gir[half(2 + i), :].astype(F32)).astype(BF16)
                 z_own[i].start()
 
-    pl.semaphore_wait(barrier, 3 + has_next.astype(jnp.int32))
-    for n in range(PARTS):
-        for d in range(2):
-            go(gather[d][n])
-    start_if(True, z_img[:2])
-    start_if(has_next, next_own[:2])
     for copy in local[:3]:
         copy.wait()
     meta[0] = jnp.zeros((8, ROWS), F32)
     meta[0, 0:1, :] = vecs[0].astype(F32)
     meta[0, 1:2, :] = pairs[...].astype(F32)
     col[0] = jnp.broadcast_to(vecs[1].astype(F32), (8, ROWS))
-    start_if(True, z_img[2:])
-    start_if(has_next, next_own[2:])
-    for d in range(2):
-        go(cols[d][0])
+    greeted = sum(they_first.astype(jnp.int32) for they_first, _, _, _, _ in meets)
+
+    @pl.when(greeted > 0)
+    def _():
+        pl.semaphore_wait(barrier, greeted)
+
+    for they_first, _, grp, blk, sem in meets:
+        if sem is not None:
+
+            @pl.when(they_first)
+            def _(grp=grp, blk=blk, sem=sem):
+                greet(grp, blk, ready.at[sem])
+
+    def open_side(condition, d, answer):
+        @pl.when(condition)
+        def _():
+            if answer:
+                pl.semaphore_wait(ready.at[1 - d], 1)
+            cols[d][0].start()
+            for n in range(PARTS):
+                gather[d][n].start()
+
+    open_side(left_first, 1, False)
+    open_side(right_first, 0, False)
+    open_side(no(right_first), 0, True)
+    open_side(no(left_first), 1, True)
+    beside = lax.rem(b, RUN) == RUN - 2
+    held = jnp.logical_or(beside, both(both(zero, y == 0), high))
+
+    def open_z(condition):
+        @pl.when(condition)
+        def _():
+            @pl.when(no(z_first))
+            def _():
+                pl.semaphore_wait(ready.at[2], 1)
+
+            for copy in z_img:
+                copy.start()
+
+    open_z(no(held))
+
+    @pl.when(has_next)
+    def _():
+        @pl.when(no(next_first))
+        def _():
+            pl.semaphore_wait(ready.at[3], 1)
+
+        for copy in next_own:
+            copy.start()
+
     for copy in local[3:]:
         copy.wait()
     columns(0)
-    arrived(0, 1)
+    arrived(0)
 
     @pl.when(outlet)
     def _():
-        for got, copy in zip(z_img, next_other):
+        z_img[0].wait_recv()
+        next_other[0].start()
+
+    arrived(1)
+    open_z(held)
+
+    @pl.when(outlet)
+    def _():
+        for got, copy in zip(z_img[1:], next_other[1:]):
             got.wait_recv()
             copy.start()
 
     arrived(2)
-    pass_on(jnp.logical_and(inlet, jnp.logical_not(zero)), 3)
+    pass_on(both(inlet, no(zero)), 3)
     arrived(3)
 
-    @pl.when(jnp.logical_not(outlet))
-    def _():
-        for copy in z_img:
-            copy.wait_recv()
-
-    start_if(jnp.logical_not(last), next_other)
+    def z_arrived(condition):
+        @pl.when(condition)
+        def _():
+            for copy in z_img:
+                copy.wait_recv()
+
+            @pl.when(no(last))
+            def _():
+                for copy in next_other:
+                    copy.start()
+
+    z_arrived(no(jnp.logical_or(outlet, beside)))
     turn(0)
-    turn(1)
     columns(1, 2)
     arrived(4)
-    pass_on(jnp.logical_and(inlet, jnp.logical_not(zero)), 2)
-    arrived(5, 6, 7)
-    pass_on(jnp.logical_and(inlet, zero), 3)
+    pass_on(both(inlet, no(zero)), 2)
+    arrived(5)
+    z_arrived(beside)
+    turn(1)
+    arrived(6, 7)
+    pass_on(both(inlet, zero), 3)
+    pass_on(both(origin, y == 0), 2)
     columns(3, 4)
     arrived(8, 9)
-    pass_on(jnp.logical_and(inlet, zero), 2)
+    pass_on(both(origin, y > 0), 2)
     near = sorted([(5, part) for part in FAR[0]] + [(6, part) for part in FAR[1]])
     far = sorted([(5, part) for part in FAR[1]] + [(6, part) for part in FAR[0]])
 
@@ -375,19 +446,24 @@
     contribution(far)
     reduce_step(5, 6)
     contribution(whole(1, 2))
+    inlet_back(no(zero), 0)
     g0[...] = image_term(0)
     contribution(whole(0))
+    inlet_back(no(zero), 1)
     reduce_step(7, 8)
-    own_back(jnp.logical_not(last))
-    inlet_back(0)
+    inlet_back(no(zero), 2)
+    inlet_back(no(zero), 3)
+    own_back(no(last), 0, 1)
     reduce_step(9)
-    inlet_back(1)
+    inlet_back(zero, 0)
     reduce_step(10)
-    inlet_back(2)
+    inlet_back(zero, 1)
     reduce_step(11)
-    inlet_back(3)
+    inlet_back(zero, 2)
+    own_back(last, 0)
     reduce_step(12, 13)
-    own_back(last)
+    inlet_back(zero, 3)
+    own_back(last, 1)
 
     @pl.when(has_next)
     def _():
@@ -468,6 +544,7 @@
             pltpu.VMEM((ROWS, width), BF16),
             pltpu.VMEM((2, 1, ROWS), BF16),
             pltpu.VMEM((1, ROWS), jnp.int32),
+            pltpu.SemaphoreType.REGULAR((4,)),
             dma((5,)),
             dma,
             dma,

time: 52.9 us -> 52.3 us (0.989)
    pallas_call x1, Pallas kernels: 50.6 us -> 50 us  [body(): pl.pallas_call(kernel, out_shape=(out, out), in_specs=[hbm, hbm, pl.Block...]
where the time goes in v4:
time: 52.3 us; the launch traced here: 52.1 us
  Pallas kernels  50.9 us (97%)
  between operations  1.28 us (2%)
    pallas_call x1, Pallas kernels, body(): pl.pallas_call(kernel, out_shape=(out, out), in_specs=[hbm, hbm, pl.Block...  50 us

profile of v4, /device:TPU:64, one launch (start us, length us, event | category | flops | bytes accessed | tf_op | source)
XLA Modules:
  0.0 52.1 jit_solution(3313362837263154124)
XLA Ops:
  1.3 50.0 %shard_map.77 = (bf16[1,128,1024]{2,1,0:T(8,128)(2,1)S(1)}, bf16[1,128,1024]{2,1,0:T(8,128)(2,1)S(1)}) custom-call(bf16[1,128,1024]{2,1,0:T(8,128)(2,1)} %image.1, bf16[1,128,1024]{2,1,0:T(8,128)(2,1)} %text.1, f32[1]{0:T(128)} %bitcast.1.scale_ref, bf16[1,128]{1,0:T(2,128)(2,1)} %lrow_ref.1, bf16[1,128]{1,0:T(2,128)(2,1)} %lcol_ref.1, s32[1,128]{1,0:T(1,128)} %pair_ref.1), custom_call_target="tpu_custom_call" | custom-call | flops 3221225472 | bytes 1048576 | tf_op jit(solution)/shard_map/pallas_call | solution.py:523
  51.3 0.8 %shard_map.78 = (bf16[1,128,1024]{2,1,0:T(8,128)(2,1)}, bf16[1,128,1024]{2,1,0:T(8,128)(2,1)}) custom-call(bf16[1,128,1024]{2,1,0:T(8,128)(2,1)S(1)} %get-tuple-element.4.gi, bf16[1,128,1024]{2,1,0:T(8,128)(2,1)S(1)} %get-tuple-element.5.gt), custom_call_target="tpu_custom_call" | custom-call | tf_op jit(solution)/shard_map/pallas_call | solution.py:570

commit v5 on v4

--- a/solution.py
+++ b/solution.py
@@ -36,7 +36,7 @@
     n0, n1 = FAR[1 - direction][:STEP], FAR[1 - direction][STEP:]
     order = [
         (3, n0), (3, n1), (4, f0), (4, f1), (2, n0), (3, f0), (3, f1),
-        (2, n1), (2, f0), (2, f1), (1, n0), (1, f0), (1, f1), (1, n1),
+        (2, n1), (2, f0), (2, f1), (1, n0), (1, n1), (1, f0), (1, f1),
     ]
     return [(hops, part) for hops, parts in order for part in parts]
 
@@ -73,15 +73,18 @@
     origin = both(zero, low)
     left_first = jnp.where(y == 0, origin, both(y < 7, no(both(origin, y == 1))))
     right_first = jnp.where(y == 0, origin, jnp.where(y == 7, no(origin), y == 6))
-    z_first = jnp.where(both(zero, y == 0), low, high)
-    prev_first = both(has_prev, no(zero))
-    next_first = both(has_next, nxt == 0)
+    z_first = jnp.where(jnp.logical_or(both(zero, y == 0), nxt == 0), low, high)
+    prev_first = both(has_prev, no(jnp.logical_or(zero, both(b == 1, both(y == 0, low)))))
+    next_first = both(has_next, jnp.logical_or(nxt == 0, both(origin, y == 0)))
+    direct_from = both(both(zero, y == 0), high)
+    direct_to = both(both(nxt == 0, y == 0), outlet)
     meets = (
         (left_first, True, side[1], b, 1),
         (right_first, True, side[0], b, 0),
         (z_first, True, zpart, b, 2),
         (prev_first, has_prev, prev_grp, prv, 3),
         (next_first, has_next, next_grp, nxt, None),
+        (direct_to, both(direct_from, True), g, prv, None),
     )
     barrier = pltpu.get_barrier_semaphore()
 
@@ -162,6 +165,7 @@
     next_own = image_copies(0, 2 + swap, 1, grp=next_grp, blk=nxt)
     next_other = image_copies(1, 3 - swap, 2, grp=next_grp, blk=nxt)
     passed = {3: image_copies(3, 2, 3, grp=zpart), 2: image_copies(2, 3, 4, grp=zpart)}
+    direct = image_copies(1, 3, 5, grp=g, blk=nxt)
     arrivals = {2: image_copies(0, 2, 0, grp=zpart), 3: image_copies(0, 3, 0, grp=zpart)}
 
     def image_arrived(slot):
@@ -174,12 +178,13 @@
             for copy in copies:
                 copy.start()
 
-    def pass_on(condition, slot):
+    def pass_on(condition, slot, skip=False):
         @pl.when(condition)
         def _():
             for got, copy in zip(arrivals[slot], passed[slot]):
                 got.wait_recv()
-                copy.start()
+                if not skip:
+                    copy.start()
 
     def take(ref, parts):
         pieces = []
@@ -296,24 +301,27 @@
                 zs[half(i), :] = (g0[half(2 + i), :] + gir[half(2 + i), :].astype(F32)).astype(BF16)
                 z_own[i].start()
 
+    behind = jnp.logical_or(y < 2, y == RING - 1)
+
+    greeted = sum(they_first.astype(jnp.int32) for they_first, *_ in meets)
+
+    @pl.when(greeted > 0)
+    def _():
+        pl.semaphore_wait(barrier, greeted)
+
+    for they_first, _, grp, blk, sem in meets:
+        if sem is not None:
+
+            @pl.when(they_first)
+            def _(grp=grp, blk=blk, sem=sem):
+                greet(grp, blk, ready.at[sem])
+
     for copy in local[:3]:
         copy.wait()
     meta[0] = jnp.zeros((8, ROWS), F32)
     meta[0, 0:1, :] = vecs[0].astype(F32)
     meta[0, 1:2, :] = pairs[...].astype(F32)
     col[0] = jnp.broadcast_to(vecs[1].astype(F32), (8, ROWS))
-    greeted = sum(they_first.astype(jnp.int32) for they_first, _, _, _, _ in meets)
-
-    @pl.when(greeted > 0)
-    def _():
-        pl.semaphore_wait(barrier, greeted)
-
-    for they_first, _, grp, blk, sem in meets:
-        if sem is not None:
-
-            @pl.when(they_first)
-            def _(grp=grp, blk=blk, sem=sem):
-                greet(grp, blk, ready.at[sem])
 
     def open_side(condition, d, answer):
         @pl.when(condition)
@@ -326,8 +334,6 @@
 
     open_side(left_first, 1, False)
     open_side(right_first, 0, False)
-    open_side(no(right_first), 0, True)
-    open_side(no(left_first), 1, True)
     beside = lax.rem(b, RUN) == RUN - 2
     held = jnp.logical_or(beside, both(both(zero, y == 0), high))
 
@@ -341,7 +347,10 @@
             for copy in z_img:
                 copy.start()
 
-    open_z(no(held))
+    open_z(last)
+    open_side(no(right_first), 0, True)
+    open_side(no(left_first), 1, True)
+    open_z(no(jnp.logical_or(held, last)))
 
     @pl.when(has_next)
     def _():
@@ -361,15 +370,17 @@
     def _():
         z_img[0].wait_recv()
         next_other[0].start()
+        pl.when(direct_to)(direct[0].start)
 
     arrived(1)
     open_z(held)
 
     @pl.when(outlet)
     def _():
-        for got, copy in zip(z_img[1:], next_other[1:]):
+        for got, copy, more in zip(z_img[1:], next_other[1:], direct[1:]):
             got.wait_recv()
             copy.start()
+            pl.when(direct_to)(more.start)
 
     arrived(2)
     pass_on(both(inlet, no(zero)), 3)
@@ -394,12 +405,15 @@
     arrived(5)
     z_arrived(beside)
     turn(1)
+    pass_on(both(origin, behind), 3)
     arrived(6, 7)
-    pass_on(both(inlet, zero), 3)
-    pass_on(both(origin, y == 0), 2)
+    pass_on(both(origin, no(behind)), 3)
+    pass_on(both(origin, both(behind, y > 0)), 2)
     columns(3, 4)
-    arrived(8, 9)
-    pass_on(both(origin, y > 0), 2)
+    arrived(8)
+    pass_on(both(origin, no(behind)), 2)
+    arrived(9)
+    pass_on(both(origin, y == 0), 2, skip=True)
     near = sorted([(5, part) for part in FAR[0]] + [(6, part) for part in FAR[1]])
     far = sorted([(5, part) for part in FAR[1]] + [(6, part) for part in FAR[0]])
 
@@ -424,11 +438,13 @@
     scores(opposite)
     contribution(opposite)
     reduce_step(2)
+    contribution(whole(3, 4))
+    contribution(far)
     arrived(13)
     opposite = sorted((7, part) for d in range(2) for part in FAR[d][STEP:])
     scores(opposite)
     contribution(opposite)
-    reduce_step(3)
+    reduce_step(3, 4)
     g1[...] = image_term(1)
 
     @pl.when(jnp.logical_not(inlet))
@@ -441,27 +457,24 @@
     def _():
         gir[0 : 2 * ROWS, :] = jnp.zeros((2 * ROWS, gir.shape[1]), BF16)
 
-    contribution(whole(3, 4))
-    reduce_step(4)
-    contribution(far)
-    reduce_step(5, 6)
     contribution(whole(1, 2))
-    inlet_back(no(zero), 0)
     g0[...] = image_term(0)
     contribution(whole(0))
+    reduce_step(5, 6, 7)
+    inlet_back(no(zero), 0)
     inlet_back(no(zero), 1)
-    reduce_step(7, 8)
-    inlet_back(no(zero), 2)
-    inlet_back(no(zero), 3)
+    reduce_step(8)
     own_back(no(last), 0, 1)
     reduce_step(9)
+    inlet_back(no(zero), 2)
+    reduce_step(10)
+    inlet_back(no(zero), 3)
+    reduce_step(11)
+    own_back(last, 0)
     inlet_back(zero, 0)
-    reduce_step(10)
     inlet_back(zero, 1)
-    reduce_step(11)
+    reduce_step(12, 13)
     inlet_back(zero, 2)
-    own_back(last, 0)
-    reduce_step(12, 13)
     inlet_back(zero, 3)
     own_back(last, 1)
 
@@ -502,11 +515,22 @@
 
     @pl.when(inlet)
     def _():
-        images_sent(3, 4)
+        images_sent(3)
+
+    @pl.when(both(inlet, no(both(origin, y == 0))))
+    def _():
+        images_sent(4)
+
+    @pl.when(direct_to)
+    def _():
+        images_sent(5)
 
 
 def write(gi, gt, gi_out, gt_out, sems):
-    copies = [pltpu.make_async_copy(src, dst, sems.at[i]) for i, (src, dst) in enumerate(((gi, gi_out), (gt, gt_out)))]
+    copies = [
+        pltpu.make_async_copy(src, dst, sems.at[i])
+        for i, (src, dst) in enumerate(((gi, gi_out), (gt, gt_out)))
+    ]
     for copy in copies:
         copy.start()
     for copy in copies:
@@ -549,9 +573,9 @@
             dma,
             dma,
             dma((2, msgs)),
-            dma((5,)),
             dma((6,)),
-            dma((5,)),
+            dma((6,)),
+            dma((6,)),
             dma((3,)),
             dma,
             dma((2, 4)),

time: 52.3 us -> 51 us (0.975)
  Pallas kernels: 50.9 us -> 49.5 us
    pallas_call x1, Pallas kernels: 50 us -> 48.7 us  [body(): pl.pallas_call(kernel, out_shape=(out, out), in_specs=[hbm, hbm, pl.Block...]
where the time goes in v5:
time: 51 us; the launch traced here: 50.8 us
  Pallas kernels  49.5 us (97%)
  between operations  1.28 us (3%)
    pallas_call x1, Pallas kernels, body(): pl.pallas_call(kernel, out_shape=(out, out), in_specs=[hbm, hbm, pl.Block...  48.7 us

profile of v5, /device:TPU:64, one launch (start us, length us, event | category | flops | bytes accessed | tf_op | source)
XLA Modules:
  0.0 50.8 jit_solution(15620520980314606868)
XLA Ops:
  1.3 48.7 %shard_map.77 = (bf16[1,128,1024]{2,1,0:T(8,128)(2,1)S(1)}, bf16[1,128,1024]{2,1,0:T(8,128)(2,1)S(1)}) custom-call(bf16[1,128,1024]{2,1,0:T(8,128)(2,1)} %image.1, bf16[1,128,1024]{2,1,0:T(8,128)(2,1)} %text.1, f32[1]{0:T(128)} %bitcast.1.scale_ref, bf16[1,128]{1,0:T(2,128)(2,1)} %lrow_ref.1, bf16[1,128]{1,0:T(2,128)(2,1)} %lcol_ref.1, s32[1,128]{1,0:T(1,128)} %pair_ref.1), custom_call_target="tpu_custom_call" | custom-call | flops 3221225472 | bytes 1048576 | tf_op jit(solution)/shard_map/pallas_call | solution.py:547
  50.0 0.8 %shard_map.78 = (bf16[1,128,1024]{2,1,0:T(8,128)(2,1)}, bf16[1,128,1024]{2,1,0:T(8,128)(2,1)}) custom-call(bf16[1,128,1024]{2,1,0:T(8,128)(2,1)S(1)} %get-tuple-element.4.gi, bf16[1,128,1024]{2,1,0:T(8,128)(2,1)S(1)} %get-tuple-element.5.gt), custom_call_target="tpu_custom_call" | custom-call | tf_op jit(solution)/shard_map/pallas_call | solution.py:594

commit v6 on v5

--- a/solution.py
+++ b/solution.py
@@ -74,17 +74,18 @@
     left_first = jnp.where(y == 0, origin, both(y < 7, no(both(origin, y == 1))))
     right_first = jnp.where(y == 0, origin, jnp.where(y == 7, no(origin), y == 6))
     z_first = jnp.where(jnp.logical_or(both(zero, y == 0), nxt == 0), low, high)
-    prev_first = both(has_prev, no(jnp.logical_or(zero, both(b == 1, both(y == 0, low)))))
-    next_first = both(has_next, jnp.logical_or(nxt == 0, both(origin, y == 0)))
-    direct_from = both(both(zero, y == 0), high)
-    direct_to = both(both(nxt == 0, y == 0), outlet)
+    early = lambda blk: jnp.logical_or(blk == 0, blk == n_blk - RUN)
+    prev_first = both(has_prev, no(jnp.logical_or(early(b), both(b == 1, both(y == 0, low)))))
+    next_first = both(has_next, jnp.logical_or(early(nxt), both(origin, y == 0)))
+    direct_from = both(zero, high)
+    direct_to = both(nxt == 0, low)
     meets = (
         (left_first, True, side[1], b, 1),
         (right_first, True, side[0], b, 0),
         (z_first, True, zpart, b, 2),
         (prev_first, has_prev, prev_grp, prv, 3),
         (next_first, has_next, next_grp, nxt, None),
-        (direct_to, both(direct_from, True), g, prv, None),
+        (direct_to, direct_from, zpart, prv, None),
     )
     barrier = pltpu.get_barrier_semaphore()
 
@@ -165,7 +166,7 @@
     next_own = image_copies(0, 2 + swap, 1, grp=next_grp, blk=nxt)
     next_other = image_copies(1, 3 - swap, 2, grp=next_grp, blk=nxt)
     passed = {3: image_copies(3, 2, 3, grp=zpart), 2: image_copies(2, 3, 4, grp=zpart)}
-    direct = image_copies(1, 3, 5, grp=g, blk=nxt)
+    direct = image_copies(0, 3, 5, grp=zpart, blk=nxt)
     arrivals = {2: image_copies(0, 2, 0, grp=zpart), 3: image_copies(0, 3, 0, grp=zpart)}
 
     def image_arrived(slot):
@@ -178,13 +179,12 @@
             for copy in copies:
                 copy.start()
 
-    def pass_on(condition, slot, skip=False):
+    def pass_on(condition, slot):
         @pl.when(condition)
         def _():
             for got, copy in zip(arrivals[slot], passed[slot]):
                 got.wait_recv()
-                if not skip:
-                    copy.start()
+                copy.start()
 
     def take(ref, parts):
         pieces = []
@@ -348,39 +348,42 @@
                 copy.start()
 
     open_z(last)
+
+    def open_next(condition):
+        @pl.when(both(has_next, condition))
+        def _():
+            @pl.when(no(next_first))
+            def _():
+                pl.semaphore_wait(ready.at[3], 1)
+
+            for copy in next_own:
+                copy.start()
+
+    open_next(next_first)
     open_side(no(right_first), 0, True)
     open_side(no(left_first), 1, True)
     open_z(no(jnp.logical_or(held, last)))
 
-    @pl.when(has_next)
-    def _():
-        @pl.when(no(next_first))
-        def _():
-            pl.semaphore_wait(ready.at[3], 1)
-
-        for copy in next_own:
-            copy.start()
-
+    open_next(no(next_first))
     for copy in local[3:]:
         copy.wait()
     columns(0)
     arrived(0)
+    start_if(direct_to, direct)
 
     @pl.when(outlet)
     def _():
         z_img[0].wait_recv()
         next_other[0].start()
-        pl.when(direct_to)(direct[0].start)
 
     arrived(1)
     open_z(held)
 
     @pl.when(outlet)
     def _():
-        for got, copy, more in zip(z_img[1:], next_other[1:], direct[1:]):
+        for got, copy in zip(z_img[1:], next_other[1:]):
             got.wait_recv()
             copy.start()
-            pl.when(direct_to)(more.start)
 
     arrived(2)
     pass_on(both(inlet, no(zero)), 3)
@@ -405,22 +408,23 @@
     arrived(5)
     z_arrived(beside)
     turn(1)
+    arrived(6, 7)
     pass_on(both(origin, behind), 3)
-    arrived(6, 7)
-    pass_on(both(origin, no(behind)), 3)
-    pass_on(both(origin, both(behind, y > 0)), 2)
     columns(3, 4)
     arrived(8)
-    pass_on(both(origin, no(behind)), 2)
+    pass_on(both(origin, no(behind)), 3)
     arrived(9)
-    pass_on(both(origin, y == 0), 2, skip=True)
     near = sorted([(5, part) for part in FAR[0]] + [(6, part) for part in FAR[1]])
     far = sorted([(5, part) for part in FAR[1]] + [(6, part) for part in FAR[0]])
 
-    @pl.when(jnp.logical_not(inlet))
+    @pl.when(no(inlet))
     def _():
         image_arrived(2)
         image_arrived(3)
+
+    @pl.when(origin)
+    def _():
+        image_arrived(2)
 
     turn(2)
     turn(3)
@@ -444,8 +448,16 @@
     opposite = sorted((7, part) for d in range(2) for part in FAR[d][STEP:])
     scores(opposite)
     contribution(opposite)
+    @pl.when(lax.rem(b, 2) == 1)
+    def _():
+        g1[...] = image_term(1)
+
     reduce_step(3, 4)
-    g1[...] = image_term(1)
+
+    @pl.when(lax.rem(b, 2) == 0)
+    def _():
+        g1[...] = image_term(1)
+
 
     @pl.when(jnp.logical_not(inlet))
     def _():
@@ -517,7 +529,7 @@
     def _():
         images_sent(3)
 
-    @pl.when(both(inlet, no(both(origin, y == 0))))
+    @pl.when(both(inlet, no(zero)))
     def _():
         images_sent(4)
 

time: 51 us -> 50.4 us (0.988)
    pallas_call x1, Pallas kernels: 48.7 us -> 48.2 us  [body(): pl.pallas_call(kernel, out_shape=(out, out), in_specs=[hbm, hbm, pl.Block...]
where the time goes in v6:
time: 50.4 us; the launch traced here: 50.3 us
  Pallas kernels  49 us (97%)
  between operations  1.28 us (3%)
    pallas_call x1, Pallas kernels, body(): pl.pallas_call(kernel, out_shape=(out, out), in_specs=[hbm, hbm, pl.Block...  48.2 us

profile of v6, /device:TPU:64, one launch (start us, length us, event | category | flops | bytes accessed | tf_op | source)
XLA Modules:
  0.0 50.3 jit_solution(12218539633748544475)
XLA Ops:
  1.3 48.2 %shard_map.77 = (bf16[1,128,1024]{2,1,0:T(8,128)(2,1)S(1)}, bf16[1,128,1024]{2,1,0:T(8,128)(2,1)S(1)}) custom-call(bf16[1,128,1024]{2,1,0:T(8,128)(2,1)} %image.1, bf16[1,128,1024]{2,1,0:T(8,128)(2,1)} %text.1, f32[1]{0:T(128)} %bitcast.1.scale_ref, bf16[1,128]{1,0:T(2,128)(2,1)} %lrow_ref.1, bf16[1,128]{1,0:T(2,128)(2,1)} %lcol_ref.1, s32[1,128]{1,0:T(1,128)} %pair_ref.1), custom_call_target="tpu_custom_call" | custom-call | flops 3221225472 | bytes 1048576 | tf_op jit(solution)/shard_map/pallas_call | solution.py:559
  49.5 0.8 %shard_map.78 = (bf16[1,128,1024]{2,1,0:T(8,128)(2,1)}, bf16[1,128,1024]{2,1,0:T(8,128)(2,1)}) custom-call(bf16[1,128,1024]{2,1,0:T(8,128)(2,1)S(1)} %get-tuple-element.4.gi, bf16[1,128,1024]{2,1,0:T(8,128)(2,1)S(1)} %get-tuple-element.5.gt), custom_call_target="tpu_custom_call" | custom-call | tf_op jit(solution)/shard_map/pallas_call | solution.py:606

commit v7 on v6

--- a/solution.py
+++ b/solution.py
@@ -408,12 +408,12 @@
     arrived(5)
     z_arrived(beside)
     turn(1)
-    arrived(6, 7)
+    arrived(6)
     pass_on(both(origin, behind), 3)
+    arrived(7)
+    pass_on(both(origin, no(behind)), 3)
     columns(3, 4)
-    arrived(8)
-    pass_on(both(origin, no(behind)), 3)
-    arrived(9)
+    arrived(8, 9)
     near = sorted([(5, part) for part in FAR[0]] + [(6, part) for part in FAR[1]])
     far = sorted([(5, part) for part in FAR[1]] + [(6, part) for part in FAR[0]])
 

time: 50.4 us -> 50.2 us (level)
  the two profiles are of different devices: /device:TPU:64 before, /device:TPU:326 now
where the time goes in v7:
time: 50.2 us; the launch traced here: 50.1 us
  Pallas kernels  48.8 us (97%)
  between operations  1.28 us (3%)
    pallas_call x1, Pallas kernels, body(): pl.pallas_call(kernel, out_shape=(out, out), in_specs=[hbm, hbm, pl.Block...  48 us

profile of v7, /device:TPU:326, one launch (start us, length us, event | category | flops | bytes accessed | tf_op | source)
XLA Modules:
  0.0 50.1 jit_solution(8117411995924644737)
XLA Ops:
  1.3 48.0 %shard_map.77 = (bf16[1,128,1024]{2,1,0:T(8,128)(2,1)S(1)}, bf16[1,128,1024]{2,1,0:T(8,128)(2,1)S(1)}) custom-call(bf16[1,128,1024]{2,1,0:T(8,128)(2,1)} %image.1, bf16[1,128,1024]{2,1,0:T(8,128)(2,1)} %text.1, f32[1]{0:T(128)} %bitcast.1.scale_ref, bf16[1,128]{1,0:T(2,128)(2,1)} %lrow_ref.1, bf16[1,128]{1,0:T(2,128)(2,1)} %lcol_ref.1, s32[1,128]{1,0:T(1,128)} %pair_ref.1), custom_call_target="tpu_custom_call" | custom-call | flops 3221225472 | bytes 1048576 | tf_op jit(solution)/shard_map/pallas_call | solution.py:559
  49.3 0.8 %shard_map.78 = (bf16[1,128,1024]{2,1,0:T(8,128)(2,1)}, bf16[1,128,1024]{2,1,0:T(8,128)(2,1)}) custom-call(bf16[1,128,1024]{2,1,0:T(8,128)(2,1)S(1)} %get-tuple-element.4.gi, bf16[1,128,1024]{2,1,0:T(8,128)(2,1)S(1)} %get-tuple-element.5.gt), custom_call_target="tpu_custom_call" | custom-call | tf_op jit(solution)/shard_map/pallas_call | solution.py:606

commit v8 on v7

--- a/solution.py
+++ b/solution.py
@@ -105,7 +105,7 @@
         )
 
     local = [
-        pltpu.make_async_copy(src, dst, local_sem.at[i])
+        pltpu.make_async_copy(src, dst, local_sem.at[min(i, 3)])
         for i, (src, dst) in enumerate((
             (pair_ref, pairs),
             (lrow_ref, vecs.at[0]),
@@ -152,22 +152,22 @@
                 if n + PARTS < len(orders[d]):
                     go(gather[d][n + PARTS])
 
-    def image_copies(src, dst, sem, **to):
+    def image_copies(src, dst, **to):
         def copy(i):
             start = i * HALF
             rows = image.at[0, pl.ds(start, HALF)] if src == 0 else img.at[pl.ds(src * ROWS + start, HALF)]
             r_sem = im_r.at[2 * (dst - 1) + i]
-            return copy_to(rows, img.at[pl.ds(dst * ROWS + start, HALF)], im_s.at[sem], r_sem, **to)
-
-        return copy(0), copy(1), copy_to(meta.at[src], meta.at[dst], me_s.at[sem], me_r.at[dst - 1], **to)
+            return copy_to(rows, img.at[pl.ds(dst * ROWS + start, HALF)], im_s, r_sem, **to)
+
+        return copy(0), copy(1), copy_to(meta.at[src], meta.at[dst], me_s, me_r.at[dst - 1], **to)
 
     swap = last.astype(jnp.int32)
-    z_img = image_copies(0, 1, 0, grp=zpart)
-    next_own = image_copies(0, 2 + swap, 1, grp=next_grp, blk=nxt)
-    next_other = image_copies(1, 3 - swap, 2, grp=next_grp, blk=nxt)
-    passed = {3: image_copies(3, 2, 3, grp=zpart), 2: image_copies(2, 3, 4, grp=zpart)}
-    direct = image_copies(0, 3, 5, grp=zpart, blk=nxt)
-    arrivals = {2: image_copies(0, 2, 0, grp=zpart), 3: image_copies(0, 3, 0, grp=zpart)}
+    z_img = image_copies(0, 1, grp=zpart)
+    next_own = image_copies(0, 2 + swap, grp=next_grp, blk=nxt)
+    next_other = image_copies(1, 3 - swap, grp=next_grp, blk=nxt)
+    passed = {3: image_copies(3, 2, grp=zpart), 2: image_copies(2, 3, grp=zpart)}
+    direct = image_copies(0, 3, grp=zpart, blk=nxt)
+    arrivals = {2: image_copies(0, 2, grp=zpart), 3: image_copies(0, 3, grp=zpart)}
 
     def image_arrived(slot):
         for copy in arrivals[slot]:
@@ -365,8 +365,7 @@
     open_z(no(jnp.logical_or(held, last)))
 
     open_next(no(next_first))
-    for copy in local[3:]:
-        copy.wait()
+    pltpu.make_async_copy(txt.at[pl.ds(0, 2 * ROWS)], txt.at[pl.ds(0, 2 * ROWS)], local_sem.at[3]).wait()
     columns(0)
     arrived(0)
     start_if(direct_to, direct)
@@ -448,13 +447,15 @@
     opposite = sorted((7, part) for d in range(2) for part in FAR[d][STEP:])
     scores(opposite)
     contribution(opposite)
-    @pl.when(lax.rem(b, 2) == 1)
+    held_back = both(lax.rem(b, 2) == 1, b != n_blk - RUN - 1)
+
+    @pl.when(held_back)
     def _():
         g1[...] = image_term(1)
 
     reduce_step(3, 4)
 
-    @pl.when(lax.rem(b, 2) == 0)
+    @pl.when(no(held_back))
     def _():
         g1[...] = image_term(1)
 
@@ -476,19 +477,18 @@
     inlet_back(no(zero), 0)
     inlet_back(no(zero), 1)
     reduce_step(8)
-    own_back(no(last), 0, 1)
+    own_back(no(outlet), 0, 1)
     reduce_step(9)
     inlet_back(no(zero), 2)
     reduce_step(10)
     inlet_back(no(zero), 3)
     reduce_step(11)
-    own_back(last, 0)
     inlet_back(zero, 0)
     inlet_back(zero, 1)
     reduce_step(12, 13)
     inlet_back(zero, 2)
     inlet_back(zero, 3)
-    own_back(last, 1)
+    own_back(outlet, 0, 1)
 
     @pl.when(has_next)
     def _():
@@ -509,33 +509,22 @@
     def all_sent(ref, sem):
         pltpu.make_async_copy(ref, ref, sem).wait()
 
-    def images_sent(*sems):
-        for sem in sems:
-            all_sent(img.at[pl.ds(0, ROWS)], im_s.at[sem])
-            all_sent(meta.at[0], me_s.at[sem])
+    def images_sent(condition, count):
+        @pl.when(condition)
+        def _():
+            all_sent(txt.at[pl.ds(0, count * ROWS)], im_s)
+            all_sent(col.at[pl.ds(0, count)], me_s)
 
     all_sent(rrecv, ag_s)
     all_sent(rrecv, rs_s)
     all_sent(col.at[pl.ds(0, 7)], co_s)
     all_sent(gis, gi_s)
     all_sent(zs, zz_s)
-    images_sent(0)
-
-    @pl.when(has_next)
-    def _():
-        images_sent(1, 2)
-
-    @pl.when(inlet)
-    def _():
-        images_sent(3)
-
-    @pl.when(both(inlet, no(zero)))
-    def _():
-        images_sent(4)
-
-    @pl.when(direct_to)
-    def _():
-        images_sent(5)
+    images_sent(no(jnp.logical_or(has_next, direct_to)), 1)
+    images_sent(direct_to, 2)
+    images_sent(both(has_next, no(inlet)), 3)
+    images_sent(both(inlet, zero), 4)
+    images_sent(both(inlet, no(zero)), 5)
 
 
 def write(gi, gt, gi_out, gt_out, sems):
@@ -581,13 +570,13 @@
             pltpu.VMEM((2, 1, ROWS), BF16),
             pltpu.VMEM((1, ROWS), jnp.int32),
             pltpu.SemaphoreType.REGULAR((4,)),
-            dma((5,)),
+            dma((4,)),
             dma,
             dma,
             dma((2, msgs)),
+            dma,
             dma((6,)),
-            dma((6,)),
-            dma((6,)),
+            dma,
             dma((3,)),
             dma,
             dma((2, 4)),

time: 50.2 us -> 49.9 us (level)
  the two profiles are of different devices: /device:TPU:326 before, /device:TPU:8 now
where the time goes in v8:
time: 49.9 us; the launch traced here: 49.7 us
  Pallas kernels  48.4 us (97%)
  between operations  1.28 us (3%)
    pallas_call x1, Pallas kernels, body(): pl.pallas_call(kernel, out_shape=(out, out), in_specs=[hbm, hbm, pl.Block...  47.6 us

profile of v8, /device:TPU:8, one launch (start us, length us, event | category | flops | bytes accessed | tf_op | source)
XLA Modules:
  0.0 49.7 jit_solution(12249704562108384552)
XLA Ops:
  1.3 47.6 %shard_map.77 = (bf16[1,128,1024]{2,1,0:T(8,128)(2,1)S(1)}, bf16[1,128,1024]{2,1,0:T(8,128)(2,1)S(1)}) custom-call(bf16[1,128,1024]{2,1,0:T(8,128)(2,1)} %image.1, bf16[1,128,1024]{2,1,0:T(8,128)(2,1)} %text.1, f32[1]{0:T(128)} %bitcast.1.scale_ref, bf16[1,128]{1,0:T(2,128)(2,1)} %lrow_ref.1, bf16[1,128]{1,0:T(2,128)(2,1)} %lcol_ref.1, s32[1,128]{1,0:T(1,128)} %pair_ref.1), custom_call_target="tpu_custom_call" | custom-call | flops 3221225472 | bytes 1048576 | tf_op jit(solution)/shard_map/pallas_call | solution.py:548
  48.9 0.8 %shard_map.78 = (bf16[1,128,1024]{2,1,0:T(8,128)(2,1)}, bf16[1,128,1024]{2,1,0:T(8,128)(2,1)}) custom-call(bf16[1,128,1024]{2,1,0:T(8,128)(2,1)S(1)} %get-tuple-element.4.gi, bf16[1,128,1024]{2,1,0:T(8,128)(2,1)S(1)} %get-tuple-element.5.gt), custom_call_target="tpu_custom_call" | custom-call | tf_op jit(solution)/shard_map/pallas_call | solution.py:595

commit v9 on v8

--- a/solution.py
+++ b/solution.py
@@ -416,6 +416,8 @@
     near = sorted([(5, part) for part in FAR[0]] + [(6, part) for part in FAR[1]])
     far = sorted([(5, part) for part in FAR[1]] + [(6, part) for part in FAR[0]])
 
+    columns(5, 6)
+
     @pl.when(no(inlet))
     def _():
         image_arrived(2)
@@ -428,21 +430,32 @@
     turn(2)
     turn(3)
     arrived(10)
-    columns(5, 6)
     scores(near)
     contribution(near)
     reduce_step(0, 1)
-    scores(whole(0, 1, 2, 3, 4))
+
+    @pl.when(no(zero))
+    def _():
+        scores(whole(0, 1, 2, 3, 4))
+
     arrived(11)
-    scores(far)
+
+    @pl.when(no(zero))
+    def _():
+        scores(far)
+
     arrived(12)
     columns(7)
     opposite = sorted((7, part) for d in range(2) for part in FAR[d][:STEP])
     scores(opposite)
     contribution(opposite)
     reduce_step(2)
-    contribution(whole(3, 4))
-    contribution(far)
+
+    @pl.when(no(zero))
+    def _():
+        contribution(whole(3, 4))
+        contribution(far)
+
     arrived(13)
     opposite = sorted((7, part) for d in range(2) for part in FAR[d][STEP:])
     scores(opposite)
@@ -453,7 +466,16 @@
     def _():
         g1[...] = image_term(1)
 
-    reduce_step(3, 4)
+    reduce_step(3)
+
+    @pl.when(zero)
+    def _():
+        scores(whole(0, 1, 2, 3, 4))
+        scores(far)
+        contribution(whole(3, 4))
+        contribution(far)
+
+    reduce_step(4)
 
     @pl.when(no(held_back))
     def _():

time: 49.9 us -> 49.9 us (level)
  no operation moved by 1% of the time
where the time goes in v9:
time: 49.9 us; the launch traced here: 49.7 us
  Pallas kernels  48.4 us (97%)
  between operations  1.28 us (3%)
    pallas_call x1, Pallas kernels, body(): pl.pallas_call(kernel, out_shape=(out, out), in_specs=[hbm, hbm, pl.Block...  47.6 us

profile of v9, /device:TPU:8, one launch (start us, length us, event | category | flops | bytes accessed | tf_op | source)
XLA Modules:
  0.0 49.7 jit_solution(6968438129305873663)
XLA Ops:
  1.3 47.6 %shard_map.77 = (bf16[1,128,1024]{2,1,0:T(8,128)(2,1)S(1)}, bf16[1,128,1024]{2,1,0:T(8,128)(2,1)S(1)}) custom-call(bf16[1,128,1024]{2,1,0:T(8,128)(2,1)} %image.1, bf16[1,128,1024]{2,1,0:T(8,128)(2,1)} %text.1, f32[1]{0:T(128)} %bitcast.1.scale_ref, bf16[1,128]{1,0:T(2,128)(2,1)} %lrow_ref.1, bf16[1,128]{1,0:T(2,128)(2,1)} %lcol_ref.1, s32[1,128]{1,0:T(1,128)} %pair_ref.1), custom_call_target="tpu_custom_call" | custom-call | flops 3221225472 | bytes 1048576 | tf_op jit(solution)/shard_map/pallas_call | solution.py:570
  48.9 0.8 %shard_map.78 = (bf16[1,128,1024]{2,1,0:T(8,128)(2,1)}, bf16[1,128,1024]{2,1,0:T(8,128)(2,1)}) custom-call(bf16[1,128,1024]{2,1,0:T(8,128)(2,1)S(1)} %get-tuple-element.4.gi, bf16[1,128,1024]{2,1,0:T(8,128)(2,1)S(1)} %get-tuple-element.5.gt), custom_call_target="tpu_custom_call" | custom-call | tf_op jit(solution)/shard_map/pallas_call | solution.py:617
